TPU v7x, 512 devices: a whole 4x4x16 slice. The times are simulated.
512 devices in a mesh: tm: 32 (over z, core), chan: 16 (over y, x).
Axes of the slice: x: 4, y: 4, z: 16, core: 2. Of those that a mesh axis runs over, the one named last changes fastest.
Arguments:
- latent: bfloat16 [384, 96, 416], P('chan', 'tm'), may hold values from -50 to 50
- norm_gain_one: float32 [384], P('chan'), may hold values from 0.1 to 1.9
- conv_weight_one: bfloat16 [3, 9, 384, 384], P(None, None, 'chan'), may hold values from -0.5 to 0.5
- conv_bias_one: float32 [384], P('chan'), may hold values from -3 to 3
- norm_gain_two: float32 [384], P('chan'), may hold values from 0.1 to 1.9
- conv_weight_two: bfloat16 [3, 9, 384, 384], P(None, None, 'chan'), may hold values from -0.5 to 0.5
- conv_bias_two: float32 [384], P('chan'), may hold values from -3 to 3
Outputs:
- block_out: bfloat16 [384, 96, 416], P('chan', 'tm')
All inputs are finite; a program needn't handle non-finite values.
Results may differ from a plain program's by a relative error of at most 0.0059.
Values may be sent and summed in bfloat16 or wider, within the bound.
A program may use at most 64 MiB of HBM per device.

v0:
```python
import jax
import jax.numpy as jnp
from jax import lax
from jax.sharding import PartitionSpec as P

COLS = 104
ROWS = 4


def from_behind(x, axis, by):
    size = lax.axis_size(axis)
    pairs = [(i, i + by) for i in range(size) if 0 <= i + by < size]
    return lax.ppermute(x, axis, pairs)


def activate(value, gain, chans):
    v32 = value.astype(jnp.float32)
    squares = lax.psum(jnp.sum(v32 * v32, axis=0), "chan")
    normed = v32 * lax.rsqrt(squares / chans + 1e-06)[None] * gain[:, None, None]
    return jax.nn.silu(normed).astype(jnp.bfloat16)


def spatial_stack(act):
    chans, frames, cells = act.shape
    grid = act.reshape(chans, frames, ROWS, COLS)
    padded = jnp.pad(grid, ((0, 0), (0, 0), (1, 1), (1, 1)))
    pieces = []
    for dy in range(3):
        for dx in range(3):
            pieces.append(
                padded[:, :, dy : dy + ROWS, dx : dx + COLS].reshape(chans, frames, cells)
            )
    return jnp.stack(pieces, 0)


def apply_taps(weight_part, stacked, frames):
    total = jnp.einsum(
        "sco,scfp->ofp", weight_part[0], stacked[:, :, 0:frames], preferred_element_type=jnp.float32
    )
    for k in range(1, 3):
        total = total + jnp.einsum(
            "sco,scfp->ofp",
            weight_part[k],
            stacked[:, :, k : k + frames],
            preferred_element_type=jnp.float32,
        )
    return total


def convolve(act, weight, bias):
    own_chans, frames, cells = act.shape
    earlier = from_behind(act[:, frames - 2 :], "tm", 1)
    extended = jnp.concatenate([earlier, act], axis=1)
    stacked = spatial_stack(extended)
    summed = lax.psum_scatter(
        apply_taps(weight, stacked, frames), "chan", scatter_dimension=0, tiled=True
    )
    return summed + bias[:, None, None]


def shards(
    latent,
    norm_gain_one,
    conv_weight_one,
    conv_bias_one,
    norm_gain_two,
    conv_weight_two,
    conv_bias_two,
):
    chans = float(conv_weight_one.shape[3])
    first = activate(latent, norm_gain_one, chans)
    middle = convolve(first, conv_weight_one, conv_bias_one).astype(jnp.bfloat16)
    second = activate(middle, norm_gain_two, chans)
    result = latent.astype(jnp.float32) + convolve(second, conv_weight_two, conv_bias_two)
    return result.astype(jnp.bfloat16)


def solution(mesh):
    in_specs = (
        P("chan", "tm", None),
        P("chan"),
        P(None, None, "chan", None),
        P("chan"),
        P("chan"),
        P(None, None, "chan", None),
        P("chan"),
    )
    out_specs = P("chan", "tm", None)
    return jax.shard_map(shards, mesh=mesh, in_specs=in_specs, out_specs=out_specs, check_vma=False)
```

profile of v0, /device:TPU:1, one launch (start us, length us, event | category | flops | bytes accessed | tf_op | source)
XLA Modules:
  0.0 376.6 jit_solution(12495691904773040355)
XLA Ops:
  6.5 1.0 fusion.8
  7.5 34.8 %psum.14 = f32[3,416]{1,0:T(4,128)S(1)} all-reduce(f32[3,416]{1,0:T(4,128)S(1)} %fusion.8), channel_id=1, replica_groups=mesh['tm'=32,'chan'=16] {'chan'}, use_global_device_ids=true, to_apply=%region_1.0 | all-reduce | flops 1248 | bytes 9984 | tf_op jit(solution)/shard_map/psum | solution.py:18
  42.3 1.1 fusion.13
  43.4 0.1 slice.122
  43.4 11.3 %collective-permute-start = (bf16[24,2,416]{2,1,0:T(2,128)(2,1)S(1)}, bf16[24,2,416]{2,1,0:T(2,128)(2,1)S(1)}, u32[]{:S(2)}, u32[]{:S(2)}) collective-permute-start(bf16[24,2,416]{2,1,0:T(2,128)(2,1)S(1)} %slice.122), channel_id=1, source_target_pairs={{0,16},{16,32},{32,48},{48,64},{64,80},{80,96},{96,112},{112,128},... | collective-permute-start | bytes 119816 | tf_op jit(solution)/shard_map/ppermute | solution.py:13
  54.8 1.2 collective-permute-done
  56.0 0.1 reshape.14
  56.1 0.6 pad_slice_fusion.8
  56.7 0.1 stack_reshape.62
  56.9 0.1 stack_reshape.55
  57.0 0.1 stack_reshape.56
  57.1 0.1 stack_reshape.57
  57.3 0.1 stack_reshape.59
  57.4 0.1 stack_reshape.60
  57.6 0.1 stack_reshape.61
  57.7 0.1 stack_reshape.54
  58.0 0.9 copy-done.4
  58.9 0.6 fusion.22
  59.4 0.6 fusion.24
  60.0 0.6 fusion.1
  60.6 2.9 copy.28
  63.6 0.0 all-reduce.9.cloned.1.call-start
  63.6 1.3 dynamic-slice
  65.5 124.9 %all-reduce.7.cloned.1.call-done = f32[384,3,416]{2,1,0:T(4,128)} async-done(((f32[384,3,416]{2,1,0:T(4,128)}), f32[384,3,416]{2,1,0:T(4,128)}) %all-reduce.7.cloned.1.call-update) | async-done | bytes 1916944
  190.5 1.1 fusion.2
  191.5 31.7 %psum.15 = f32[3,416]{1,0:T(4,128)S(1)} all-reduce(f32[3,416]{1,0:T(4,128)S(1)} %get-tuple-element.5), channel_id=1, replica_groups=mesh['tm'=32,'chan'=16] {'chan'}, use_global_device_ids=true, to_apply=%region_4.5 | all-reduce | flops 1248 | bytes 9984 | tf_op jit(solution)/shard_map/psum | solution.py:18
  223.2 0.2 fusion.7
  223.4 0.1 slice.123
  223.5 11.4 %collective-permute-start.1 = (bf16[24,2,416]{2,1,0:T(2,128)(2,1)S(1)}, bf16[24,2,416]{2,1,0:T(2,128)(2,1)S(1)}, u32[]{:S(2)}, u32[]{:S(2)}) collective-permute-start(bf16[24,2,416]{2,1,0:T(2,128)(2,1)S(1)} %slice.123), channel_id=1, source_target_pairs={{0,16},{16,32},{32,48},{48,64},{64,80},{80,96},{96,112},{112,128},... | collective-permute-start | bytes 119816 | tf_op jit(solution)/shard_map/ppermute | solution.py:13
  234.9 1.2 collective-permute-done.1
  236.1 0.1 reshape.15
  236.2 0.6 pad_slice_fusion
  236.8 0.1 stack_reshape.71
  236.9 0.1 stack_reshape.64
  237.1 0.1 stack_reshape.65
  237.2 0.1 stack_reshape.66
  237.4 0.1 stack_reshape.68
  237.5 0.1 stack_reshape.69
  237.6 0.1 stack_reshape.70
  237.8 0.1 stack_reshape.63
  238.1 0.9 copy-done.5
  239.0 0.6 fusion.17
  239.5 0.6 fusion.19
  240.1 0.6 fusion
  240.7 2.9 copy.31
  243.6 124.5 %all-reduce.9.cloned.1.call-done = f32[384,3,416]{2,1,0:T(4,128)} async-done(((f32[384,3,416]{2,1,0:T(4,128)}), f32[384,3,416]{2,1,0:T(4,128)}) %all-reduce.9.cloned.1.call-update) | async-done | bytes 1916944
  368.1 1.0 fusion.14
  369.2 0.7 copy.32
  (37 shorter events, 0.3 us)
Async XLA Ops:
  6.5 183.9 %all-reduce.7.cloned.1.call-start = ((), (), s32[]{:S(2)}) async-start(), calls=%async_computation | async-start | bytes 6291456
  43.4 12.5 %collective-permute-start = (bf16[24,2,416]{2,1,0:T(2,128)(2,1)S(1)}, bf16[24,2,416]{2,1,0:T(2,128)(2,1)S(1)}, u32[]{:S(2)}, u32[]{:S(2)}) collective-permute-start(bf16[24,2,416]{2,1,0:T(2,128)(2,1)S(1)} %slice.122), channel_id=1, source_target_pairs={{0,16},{16,32},{32,48},{48,64},{64,80},{80,96},{96,112},{112,128},... | collective-permute-start | bytes 119816 | tf_op jit(solution)/shard_map/ppermute | solution.py:13
  57.8 1.0 copy-start.4
  63.5 126.9 %copy-start.1 = (f32[24]{0:T(128)S(1)}, f32[24]{0:T(128)}, u32[]{:S(2)}) copy-start(f32[24]{0:T(128)} %param.10) | copy-start | bytes 292
  63.5 159.7 %copy-start.2 = (f32[24]{0:T(128)S(1)}, f32[24]{0:T(128)}, u32[]{:S(2)}) copy-start(f32[24]{0:T(128)} %param.11) | copy-start | bytes 292
  63.6 304.5 %all-reduce.9.cloned.1.call-start = ((), (), s32[]{:S(2)}) async-start(), calls=%async_computation.1 | async-start | bytes 6291456
  223.5 12.5 %collective-permute-start.1 = (bf16[24,2,416]{2,1,0:T(2,128)(2,1)S(1)}, bf16[24,2,416]{2,1,0:T(2,128)(2,1)S(1)}, u32[]{:S(2)}, u32[]{:S(2)}) collective-permute-start(bf16[24,2,416]{2,1,0:T(2,128)(2,1)S(1)} %slice.123), channel_id=1, source_target_pairs={{0,16},{16,32},{32,48},{48,64},{64,80},{80,96},{96,112},{112,128},... | collective-permute-start | bytes 119816 | tf_op jit(solution)/shard_map/ppermute | solution.py:13
  237.9 1.0 copy-start.5
  243.6 124.5 %copy-start = (bf16[24,3,416]{2,0,1:T(8,128)(2,1)S(1)}, bf16[24,3,416]{2,0,1:T(8,128)(2,1)}, u32[]{:S(2)}) copy-start(bf16[24,3,416]{2,0,1:T(8,128)(2,1)} %param.7) | copy-start | bytes 179716
  243.6 124.5 %copy-start.3 = (f32[24]{0:T(128)S(1)}, f32[24]{0:T(128)}, u32[]{:S(2)}) copy-start(f32[24]{0:T(128)} %param.13) | copy-start | bytes 292
Sparse Core Ops, SparseCore 0:
  63.7 126.7 all-reduce.6
  243.8 124.2 all-reduce.8
where the time goes:
time: 377 us
  waiting for transfers between devices  252 us (67%)
  blocking collectives  66.4 us (18%)
  starting transfers between devices  22.8 us (6%)
  between operations  14.5 us (4%)
  local copies, waits for them, and re-layouts  13.4 us (4%)
  other arithmetic  4.35 us (1%)
    unnamed x4, waiting for transfers between devices  249 us
    psum x2, blocking collectives, activate(): squares = lax.psum(jnp.sum(v32 * v32, axis=0), 'chan')  66.4 us
    ppermute x2, starting transfers between devices, from_behind(): return lax.ppermute(x, axis, pairs)  22.7 us
  transfers between devices with their start and end apart: 4, of which 4 were waited for; matrix products, arithmetic and copies ran while one was open for 0% of the time, Pallas kernels for 0%

commit v1 on v0

v1 whole, which is shorter than its diff:
```python
import functools

import jax
import jax.numpy as jnp
from jax import lax
from jax.experimental import pallas as pl
from jax.experimental.pallas import tpu as pltpu
from jax.sharding import PartitionSpec as P

COLS = 104
ROWS = 4
LANES = 128
WIDE = ROWS * LANES
SIDE = 4
OWN = 24
HALF = WIDE // 2
DEPTH = 256
F32 = jnp.float32
BF16 = jnp.bfloat16


def unfold(value):
    value = value.astype(F32)
    return jnp.concatenate([value[:OWN], value[OWN:]], axis=1)


def fold(value):
    return jnp.concatenate([value[:, :HALF], value[:, HALF:]], axis=0).astype(BF16)


def tile4(value):
    return jnp.concatenate([value] * ROWS, axis=1)


def lane_ids(rows):
    return lax.broadcasted_iota(jnp.int32, (rows, LANES), 1)


def spread(frame):
    flat = jnp.concatenate([frame, jnp.zeros((OWN, WIDE - ROWS * COLS), F32)], axis=1)
    lane = lane_ids(OWN)
    rows = []
    for row in range(ROWS):
        at, off = divmod(row * COLS, LANES)
        piece = flat[:, at * LANES : (at + 1) * LANES]
        if off:
            after = flat[:, (at + 1) * LANES : (at + 2) * LANES]
            piece = jnp.where(
                lane < LANES - off,
                pltpu.roll(piece, LANES - off, 1),
                pltpu.roll(after, LANES - off, 1),
            )
        rows.append(jnp.where(lane < COLS, piece, 0.0))
    return jnp.concatenate(rows, axis=1)


def squeeze(frame):
    lane = lane_ids(OWN)
    rows = [frame[:, r * LANES : (r + 1) * LANES] for r in range(ROWS)]
    pieces = []
    for at in range(ROWS):
        row, off = divmod(at * LANES, COLS)
        piece = rows[row]
        if off:
            piece = pltpu.roll(piece, LANES - off, 1)
        if row + 1 < ROWS:
            piece = jnp.where(lane < COLS - off, piece, pltpu.roll(rows[row + 1], COLS - off, 1))
        pieces.append(piece)
    return jnp.concatenate(pieces, axis=1)[:, : ROWS * COLS]


def kernel(
    sections,
    chans,
    lat_hbm,
    w1_hbm,
    w2_hbm,
    g1_hbm,
    b1_hbm,
    g2_hbm,
    b2_hbm,
    out_ref,
    lat,
    weights,
    vecs,
    flipped,
    gains,
    values,
    partial_a,
    partial_b,
    w_out,
    w_in,
    stacked,
    sums,
    own_sums,
    shares,
    from_line,
    from_before,
    local_sem,
    gain_send,
    gain_recv,
    value_send,
    value_recv,
    pa_send,
    pa_recv,
    pb_send,
    pb_recv,
    w_send,
    w_recv,
    line_send,
    line_recv,
    next_send,
    next_recv,
):
    t = lax.axis_index("tm")
    chan = lax.axis_index("chan")
    x, y = lax.rem(chan, SIDE), lax.div(chan, SIDE)
    parity = lax.rem(t, 2)

    swap = [parity, 1 - parity]
    index_a = [x + s * (y - x) for s in swap]
    index_b = [y + s * (x - y) for s in swap]

    def chan_at(j, a, b):
        s = swap[j]
        return a * (1 + (SIDE - 1) * s) + b * (SIDE - (SIDE - 1) * s)

    def shifted(index, d):
        return lax.rem(index + d, SIDE)

    def a_peer(j, d):
        return (t, chan_at(j, shifted(index_a[j], d), index_b[j]))

    def b_peer(j, d, later=0):
        return (t + later, chan_at(j, index_a[j], shifted(index_b[j], d)))

    def remote(src, dst, send, recv, device):
        return pltpu.make_async_remote_copy(
            src_ref=src,
            dst_ref=dst,
            send_sem=send,
            recv_sem=recv,
            device_id=device,
            device_id_type=pl.DeviceIdType.MESH,
        )

    far_first = (2, 1, 3)

    loads = [
        pltpu.make_async_copy(lat_hbm, lat, local_sem.at[0]),
        pltpu.make_async_copy(w1_hbm, weights.at[0], local_sem.at[1]),
        pltpu.make_async_copy(w2_hbm, weights.at[1], local_sem.at[2]),
    ]
    for n, ref in enumerate((g1_hbm, b1_hbm, g2_hbm, b2_hbm)):
        loads.append(pltpu.make_async_copy(ref, vecs.at[n], local_sem.at[3 + n]))
    for load in loads:
        load.start()

    barrier = pltpu.get_barrier_semaphore()

    def greet(device):
        pl.semaphore_signal(barrier, inc=1, device_id=device, device_id_type=pl.DeviceIdType.MESH)

    for d in range(1, SIDE):
        greet((t, SIDE * y + shifted(x, d)))
        greet((t, SIDE * shifted(y, d) + x))

    @pl.when(t > 0)
    def _():
        greet((t - 1, chan))
        for d in range(1, SIDE):
            greet((t - 1, SIDE * y + shifted(x, d)))
            greet((t - 1, SIDE * shifted(y, d) + x))

    def own_squares(j, f, value):
        squares = jnp.sum(value * value, axis=0, keepdims=True)
        partial_a[j, 0, 2 * f : 2 * f + 1, :] = squares[:, :HALF]
        partial_a[j, 0, 2 * f + 1 : 2 * f + 2, :] = squares[:, HALF:]

    for j in range(2):
        partial_a[j, 0] = jnp.zeros((8, HALF), F32)
    loads[0].wait()
    for f in range(3):
        value = spread(lat[f].astype(F32))
        values[0, 0, f] = fold(value)
        own_squares(0, f, value)

    for n in range(4):
        loads[3 + n].wait()
    lane = lane_ids(8)
    flipped[...] = jnp.zeros((LANES, LANES), F32)
    for n in range(4):
        flipped[n : n + 1, 0:OWN] = vecs[n]
    columns = jnp.transpose(flipped[...])[:OWN]

    def column(n):
        return jnp.broadcast_to(columns[:, n : n + 1], (OWN, LANES))

    bias = [column(1), column(3)]
    gains[0, 0] = column(0)
    gains[1, 0] = column(2)

    pl.semaphore_wait(barrier, 2 * (SIDE - 1) + jnp.where(t < sections - 1, 2 * SIDE - 1, 0))

    sends = []

    def start(copy):
        copy.start()
        sends.append(copy)

    def send_squares_a(j):
        for d in far_first:
            start(
                remote(
                    partial_a.at[j, 0],
                    partial_a.at[j, SIDE - d],
                    pa_send.at[j, d],
                    pa_recv.at[j, SIDE - d],
                    b_peer(j, d),
                )
            )

    def send_values(j):
        for d in far_first:
            start(
                remote(
                    values.at[j, 0],
                    values.at[j, SIDE - d],
                    value_send.at[j, d],
                    value_recv.at[j, SIDE - d],
                    a_peer(j, d),
                )
            )

    def send_squares_b(j):
        total = partial_a[j, 0]
        for d in (1, 3, 2):
            remote(
                partial_a.at[j, 0], partial_a.at[j, d], pa_send.at[j, d], pa_recv.at[j, d], b_peer(j, d)
            ).wait_recv()
            total = total + partial_a[j, d]
        partial_b[j, 0] = total
        for d in far_first:
            start(
                remote(
                    partial_b.at[j, 0],
                    partial_b.at[j, SIDE - d],
                    pb_send.at[j, d],
                    pb_recv.at[j, SIDE - d],
                    a_peer(j, d),
                )
            )

    def scales(j):
        total = partial_b[j, 0]
        for d in (1, 3, 2):
            remote(
                partial_b.at[j, 0], partial_b.at[j, d], pb_send.at[j, d], pb_recv.at[j, d], a_peer(j, d)
            ).wait_recv()
            total = total + partial_b[j, d]
        return lax.rsqrt(total / chans + 1e-06)

    def turn_weights(j):
        loads[1 + j].wait()
        for k in range(3):
            part = weights[j, 9 * k : 9 * k + 9].astype(F32).reshape(9 * OWN, chans)
            part = jnp.concatenate([part, jnp.zeros((DEPTH - 9 * OWN, chans), F32)], axis=0)
            flat = jnp.transpose(part)
            sums[0:chans, 0:DEPTH] = flat
            for d in range(SIDE):
                rows = []
                for e in range(SIDE):
                    block = chan_at(j, shifted(index_a[j], d), shifted(index_b[j], e))
                    rows.append(sums[pl.ds(pl.multiple_of(block * OWN, 8), OWN), 0:DEPTH])
                rows = jnp.concatenate(rows, axis=0).astype(BF16)
                if d == 0:
                    w_in[j, 0, k] = rows
                else:
                    w_out[j, d - 1, k] = rows

    def send_weights(j):
        for d in far_first:
            start(
                remote(
                    w_out.at[j, d - 1],
                    w_in.at[j, SIDE - d],
                    w_send.at[j, d],
                    w_recv.at[j, SIDE - d],
                    a_peer(j, d),
                )
            )

    def send_gains(j):
        for d in far_first:
            start(
                remote(
                    gains.at[j, 0],
                    gains.at[j, SIDE - d],
                    gain_send.at[j, d],
                    gain_recv.at[j, SIDE - d],
                    a_peer(j, d),
                )
            )

    def stack_taps(slot, j, scale):
        gain = tile4(gains[j, slot])
        for f in range(3):
            value = unfold(values[j, slot, f])
            row = jnp.concatenate([scale[2 * f : 2 * f + 1], scale[2 * f + 1 : 2 * f + 2]], axis=1)
            normed = value * row * gain
            act = 0.5 * normed * (1.0 + jnp.tanh(0.5 * normed))
            act = act.astype(BF16).astype(F32)
            rows = [act[:, r * LANES : (r + 1) * LANES] for r in range(ROWS)]
            shifts = [
                [pltpu.roll(r, 1, 1) for r in rows],
                rows,
                [pltpu.roll(r, LANES - 1, 1) for r in rows],
            ]
            none = jnp.zeros((OWN, LANES), F32)
            taps = []
            for dy in range(3):
                for dx in range(3):
                    moved = [none] + shifts[dx] + [none]
                    taps.append(jnp.concatenate(moved[dy : dy + ROWS], axis=1))
            taps.append(jnp.zeros((DEPTH - 9 * OWN, WIDE), F32))
            stacked[f, slot] = jnp.concatenate(taps, axis=0).astype(BF16)

    def convolve(j):
        left = jnp.concatenate([w_in[j, s].reshape(3 * SIDE * OWN, DEPTH) for s in range(SIDE)], axis=1)
        group = SIDE * OWN

        def emit(frame, total):
            for e in range(SIDE):
                piece = total[e * OWN : (e + 1) * OWN]
                if e == 0 and frame < 3:
                    own_sums[frame] = piece
                else:
                    shares[j, e, frame] = fold(piece)

        def product(f):
            return jnp.dot(left, stacked[f].reshape(SIDE * DEPTH, WIDE), preferred_element_type=F32)

        last = product(2)
        emit(4, last[:group])
        sums[0:group, :] = last[group : 2 * group]
        sums[group : 2 * group, :] = last[2 * group :]
        mid = product(1)
        emit(3, sums[0:group, :] + mid[:group])
        sums[group : 2 * group, :] += mid[group : 2 * group]
        sums[0:group, :] = mid[2 * group :]

        @pl.when(t < sections - 1)
        def _():
            for e in range(SIDE):
                next_copy(j, e).start()

        first = product(0)
        emit(2, sums[group : 2 * group, :] + first[:group])
        emit(1, sums[0:group, :] + first[group : 2 * group])
        emit(0, first[2 * group :])
        for d in far_first:
            start(line_copy(j, d))

    def next_copy(j, e):
        return remote(
            shares.at[j, e, pl.ds(3, 2)],
            from_before.at[j, e],
            next_send.at[j, e],
            next_recv.at[j, e],
            b_peer(j, e, 1),
        )

    def line_copy(j, d):
        return remote(
            shares.at[j, d, pl.ds(0, 3)],
            from_line.at[j, SIDE - d],
            line_send.at[j, d],
            line_recv.at[j, SIDE - d],
            b_peer(j, d),
        )

    def collect(j):
        @pl.when(t > 0)
        def _():
            for e in range(SIDE):
                remote(
                    from_before.at[j, e],
                    from_before.at[j, e],
                    next_send.at[j, e],
                    next_recv.at[j, e],
                    (t, chan_at(j, shifted(index_a[j], 1), index_b[j])),
                ).wait_recv()

        for d in (1, 3, 2):
            remote(
                from_line.at[j, d],
                from_line.at[j, d],
                line_send.at[j, d],
                line_recv.at[j, d],
                b_peer(j, d),
            ).wait_recv()
        frames = []
        for f in range(3):
            total = own_sums[f] + tile4(bias[j])
            for d in range(1, SIDE):
                total = total + unfold(from_line[j, d, f])
            if f < 2:
                for e in range(SIDE):
                    total = total + unfold(from_before[j, e, f])
            frames.append(total)
        return frames

    @pl.when(t == 0)
    def _():
        from_before[...] = jnp.zeros(from_before.shape, BF16)

    send_squares_a(0)
    send_values(0)
    send_gains(0)
    send_gains(1)
    turn_weights(0)
    send_weights(0)
    send_squares_b(0)
    turn_weights(1)
    scale = scales(0)
    for slot in (0, 1, 3, 2):
        if slot:
            remote(
                values.at[0, 0], values.at[0, slot], value_send.at[0, slot], value_recv.at[0, slot], a_peer(0, slot)
            ).wait_recv()
            remote(
                gains.at[0, 0], gains.at[0, slot], gain_send.at[0, slot], gain_recv.at[0, slot], a_peer(0, slot)
            ).wait_recv()
        stack_taps(slot, 0, scale)
    for slot in (1, 3, 2):
        remote(
            w_out.at[0, 0], w_in.at[0, slot], w_send.at[0, slot], w_recv.at[0, slot], a_peer(0, slot)
        ).wait_recv()
    send_weights(1)
    convolve(0)

    frames = collect(0)
    keep = tile4(lane_ids(OWN)) < COLS
    for f in range(3):
        middle = jnp.where(keep, frames[f], 0.0).astype(BF16).astype(F32)
        values[1, 0, f] = fold(middle)
        own_squares(1, f, middle)
    send_squares_a(1)
    send_values(1)
    send_squares_b(1)
    scale = scales(1)
    for slot in (0, 1, 3, 2):
        if slot:
            remote(
                gains.at[1, 0], gains.at[1, slot], gain_send.at[1, slot], gain_recv.at[1, slot], a_peer(1, slot)
            ).wait_recv()
            remote(
                values.at[1, 0], values.at[1, slot], value_send.at[1, slot], value_recv.at[1, slot], a_peer(1, slot)
            ).wait_recv()
        stack_taps(slot, 1, scale)
    for slot in (1, 3, 2):
        remote(
            w_out.at[1, 0], w_in.at[1, slot], w_send.at[1, slot], w_recv.at[1, slot], a_peer(1, slot)
        ).wait_recv()
    convolve(1)
    frames = collect(1)
    for f in range(3):
        out_ref[f] = (lat[f].astype(F32) + squeeze(frames[f])).astype(BF16)

    for copy in sends:
        copy.wait_send()

    @pl.when(t < sections - 1)
    def _():
        for j in range(2):
            for e in range(SIDE):
                next_copy(j, e).wait_send()


def block(sections, latent, gain_one, weight_one, bias_one, gain_two, weight_two, bias_two):
    frames = latent.shape[1]
    chans = weight_one.shape[3]
    dma = pltpu.SemaphoreType.DMA
    anywhere = pl.BlockSpec(memory_space=pl.ANY)
    result = pl.pallas_call(
        functools.partial(kernel, sections, chans),
        out_shape=jax.ShapeDtypeStruct((frames, OWN, ROWS * COLS), BF16),
        in_specs=[anywhere] * 7,
        out_specs=pl.BlockSpec(memory_space=pltpu.VMEM),
        scratch_shapes=[
            pltpu.VMEM((frames, OWN, ROWS * COLS), BF16),
            pltpu.VMEM((2, 27, OWN, chans), BF16),
            pltpu.VMEM((4, 1, OWN), F32),
            pltpu.VMEM((LANES, LANES), F32),
            pltpu.VMEM((2, SIDE, OWN, LANES), F32),
            pltpu.VMEM((2, SIDE, frames, 2 * OWN, HALF), BF16),
            pltpu.VMEM((2, SIDE, 8, HALF), F32),
            pltpu.VMEM((2, SIDE, 8, HALF), F32),
            pltpu.VMEM((2, SIDE - 1, 3, SIDE * OWN, DEPTH), BF16),
            pltpu.VMEM((2, SIDE, 3, SIDE * OWN, DEPTH), BF16),
            pltpu.VMEM((frames, SIDE, DEPTH, WIDE), BF16),
            pltpu.VMEM((chans, WIDE), F32),
            pltpu.VMEM((frames, OWN, WIDE), F32),
            pltpu.VMEM((2, SIDE, frames + 2, 2 * OWN, HALF), BF16),
            pltpu.VMEM((2, SIDE, frames, 2 * OWN, HALF), BF16),
            pltpu.VMEM((2, SIDE, 2, 2 * OWN, HALF), BF16),
            dma((7,)),
        ]
        + [dma((2, SIDE))] * 14,
        compiler_params=pltpu.CompilerParams(
            collective_id=0, has_side_effects=True, vmem_limit_bytes=40 * 1024 * 1024
        ),
    )(
        jnp.transpose(latent, (1, 0, 2)),
        weight_one.reshape(27, OWN, chans),
        weight_two.reshape(27, OWN, chans),
        gain_one.reshape(1, OWN),
        bias_one.reshape(1, OWN),
        gain_two.reshape(1, OWN),
        bias_two.reshape(1, OWN),
    )
    return jnp.transpose(result, (1, 0, 2))


def solution(mesh):
    in_specs = (
        P("chan", "tm", None),
        P("chan"),
        P(None, None, "chan", None),
        P("chan"),
        P("chan"),
        P(None, None, "chan", None),
        P("chan"),
    )
    return jax.shard_map(
        functools.partial(block, mesh.shape["tm"]),
        mesh=mesh,
        in_specs=in_specs,
        out_specs=P("chan", "tm", None),
        check_vma=False,
    )
```

time: 377 us -> 45.6 us (0.12)
  waiting for transfers between devices: 252 us -> 0 us
  blocking collectives: 66.4 us -> 0 us
  Pallas kernels: 0 us -> 41 us
  starting transfers between devices: 22.8 us -> 0 us
  between operations: 14.5 us -> 0.03 us
  local copies, waits for them, and re-layouts: 13.4 us -> 4.27 us
  other arithmetic: 4.35 us -> 0 us
    unnamed x4 -> x0, waiting for transfers between devices: 249 us -> none
    psum x2 -> x0, blocking collectives: 66.4 us -> none  [activate(): squares = lax.psum(jnp.sum(v32 * v32, axis=0), 'chan')]
    pallas_call x0 -> x1, Pallas kernels: none -> 41 us  [block(): pl.pallas_call(functools.partial(kernel, sections, chans), out_shape=jax....]
    ppermute x2 -> x0, starting transfers between devices: 22.7 us -> none  [from_behind(): return lax.ppermute(x, axis, pairs)]
    add x2 -> x0, local copies, waits for them, and re-layouts: 5.82 us -> none  [apply_taps(): total + jnp.einsum('sco,scfp->ofp', weight_part[k], stacked[:, :, k:k + f...]
  transfers between devices with their start and end apart: 4 -> 0, of which waited for: 4 -> 0; matrix products, arithmetic and copies ran while one was open for 0% -> 0% of each run, Pallas kernels for 0% -> 0%
where the time goes in v1:
time: 45.6 us; the launch traced here: 45.3 us
  Pallas kernels  41 us (90%)
  local copies, waits for them, and re-layouts  4.27 us (9%)
    pallas_call x1, Pallas kernels, block(): pl.pallas_call(functools.partial(kernel, sections, chans), out_shape=jax....  41 us
    unnamed x15, local copies, waits for them, and re-layouts  4.27 us

profile of v1, /device:TPU:1, one launch (start us, length us, event | category | flops | bytes accessed | tf_op | source)
XLA Modules:
  0.0 45.3 jit_solution(10248214064687021355)
XLA Ops:
  0.0 0.0 copy-start.6
  0.0 0.0 copy-start.3
  0.0 0.0 copy-start.4
  0.0 0.0 copy-start.5
  0.0 0.6 %copy-done.6 = f32[24]{0:T(128)S(1)} copy-done((f32[24]{0:T(128)S(1)}, f32[24]{0:T(128)}, u32[]{:S(2)}) %copy-start.6) | copy-done | bytes 120
  0.7 0.0 copy-done.3
  0.7 0.0 copy-done.4
  0.7 0.0 copy-done.5
  0.7 0.0 copy-start
  0.7 1.0 %copy-done = bf16[3,9,24,384]{3,2,1,0:T(8,128)(2,1)S(1)} copy-done((bf16[3,9,24,384]{3,2,1,0:T(8,128)(2,1)S(1)}, bf16[3,9,24,384]{3,2,1,0:T(8,128)(2,1)}, u32[]{:S(2)}) %copy-start) | copy-done | bytes 497688
  1.7 0.0 copy-start.1
  1.7 1.0 %copy-done.1 = bf16[3,9,24,384]{3,2,1,0:T(8,128)(2,1)S(1)} copy-done((bf16[3,9,24,384]{3,2,1,0:T(8,128)(2,1)S(1)}, bf16[3,9,24,384]{3,2,1,0:T(8,128)(2,1)}, u32[]{:S(2)}) %copy-start.1) | copy-done | bytes 497688
  2.8 0.0 copy-start.2
  2.8 0.9 %copy-done.2 = bf16[24,3,416]{2,0,1:T(8,128)(2,1)S(1)} copy-done((bf16[24,3,416]{2,0,1:T(8,128)(2,1)S(1)}, bf16[24,3,416]{2,0,1:T(8,128)(2,1)}, u32[]{:S(2)}) %copy-start.2) | copy-done | bytes 59928
  3.7 41.0 %shard_map.73 = bf16[3,24,416]{2,1,0:T(8,128)(2,1)S(1)} custom-call(bf16[3,24,416]{2,1,0:T(8,128)(2,1)S(1)} %bitcast.11, bf16[27,24,384]{2,1,0:T(8,128)(2,1)S(1)} %bitcast.8, bf16[27,24,384]{2,1,0:T(8,128)(2,1)S(1)} %bitcast.9, f32[1,24]{1,0:T(1,128)S(1)} %bitcast.12, f32[1,24]{1,0:T(1,128)S(1)} %bitcast.13, f32[1,24]{1,0:T(1,128)S(1)} %bitcast.14, ...), custom_call_target="tpu_custom_call" | custom-call | tf_op jit(solution)/shard_map/pallas_call | solution.py:485
  44.7 0.6 %copy.9 = bf16[24,3,416]{2,0,1:T(8,128)(2,1)} copy(bf16[24,3,416]{2,0,1:T(8,128)(2,1)S(1)} %bitcast.10) | data formatting | bytes 119808
Async XLA Ops:
  0.0 0.7 %copy-start.6 = (f32[24]{0:T(128)S(1)}, f32[24]{0:T(128)}, u32[]{:S(2)}) copy-start(f32[24]{0:T(128)} %param.13) | copy-start | bytes 292
  0.0 0.7 %copy-start.3 = (f32[24]{0:T(128)S(1)}, f32[24]{0:T(128)}, u32[]{:S(2)}) copy-start(f32[24]{0:T(128)} %param.8) | copy-start | bytes 292
  0.0 0.7 %copy-start.4 = (f32[24]{0:T(128)S(1)}, f32[24]{0:T(128)}, u32[]{:S(2)}) copy-start(f32[24]{0:T(128)} %param.10) | copy-start | bytes 292
  0.0 0.7 %copy-start.5 = (f32[24]{0:T(128)S(1)}, f32[24]{0:T(128)}, u32[]{:S(2)}) copy-start(f32[24]{0:T(128)} %param.11) | copy-start | bytes 292
  0.7 1.0 %copy-start = (bf16[3,9,24,384]{3,2,1,0:T(8,128)(2,1)S(1)}, bf16[3,9,24,384]{3,2,1,0:T(8,128)(2,1)}, u32[]{:S(2)}) copy-start(bf16[3,9,24,384]{3,2,1,0:T(8,128)(2,1)} %param.9) | copy-start | bytes 1492996
  1.7 1.0 %copy-start.1 = (bf16[3,9,24,384]{3,2,1,0:T(8,128)(2,1)S(1)}, bf16[3,9,24,384]{3,2,1,0:T(8,128)(2,1)}, u32[]{:S(2)}) copy-start(bf16[3,9,24,384]{3,2,1,0:T(8,128)(2,1)} %param.12) | copy-start | bytes 1492996
  2.8 0.9 %copy-start.2 = (bf16[24,3,416]{2,0,1:T(8,128)(2,1)S(1)}, bf16[24,3,416]{2,0,1:T(8,128)(2,1)}, u32[]{:S(2)}) copy-start(bf16[24,3,416]{2,0,1:T(8,128)(2,1)} %param.7) | copy-start | bytes 179716

commit v2 on v1

--- a/solution.py
+++ b/solution.py
@@ -84,10 +84,12 @@
     weights,
     vecs,
     flipped,
-    gains,
     values,
+    squares,
     partial_a,
     partial_b,
+    partial_all,
+    turned,
     w_out,
     w_in,
     stacked,
@@ -97,8 +99,8 @@
     from_line,
     from_before,
     local_sem,
-    gain_send,
-    gain_recv,
+    all_send,
+    all_recv,
     value_send,
     value_recv,
     pa_send,
@@ -172,22 +174,13 @@
             greet((t - 1, SIDE * y + shifted(x, d)))
             greet((t - 1, SIDE * shifted(y, d) + x))
 
-    def own_squares(j, f, value):
-        squares = jnp.sum(value * value, axis=0, keepdims=True)
-        partial_a[j, 0, 2 * f : 2 * f + 1, :] = squares[:, :HALF]
-        partial_a[j, 0, 2 * f + 1 : 2 * f + 2, :] = squares[:, HALF:]
-
-    for j in range(2):
-        partial_a[j, 0] = jnp.zeros((8, HALF), F32)
-    loads[0].wait()
-    for f in range(3):
-        value = spread(lat[f].astype(F32))
-        values[0, 0, f] = fold(value)
-        own_squares(0, f, value)
+    def own_squares(f, value):
+        sums_of = jnp.sum(value * value, axis=0, keepdims=True)
+        for r in range(ROWS):
+            squares[ROWS * f + r : ROWS * f + r + 1, :] = sums_of[:, r * LANES : (r + 1) * LANES]
 
     for n in range(4):
         loads[3 + n].wait()
-    lane = lane_ids(8)
     flipped[...] = jnp.zeros((LANES, LANES), F32)
     for n in range(4):
         flipped[n : n + 1, 0:OWN] = vecs[n]
@@ -197,10 +190,15 @@
         return jnp.broadcast_to(columns[:, n : n + 1], (OWN, LANES))
 
     bias = [column(1), column(3)]
-    gains[0, 0] = column(0)
-    gains[1, 0] = column(2)
-
-    pl.semaphore_wait(barrier, 2 * (SIDE - 1) + jnp.where(t < sections - 1, 2 * SIDE - 1, 0))
+    gain = [tile4(column(0)), tile4(column(2))]
+
+    squares[...] = jnp.zeros((16, LANES), F32)
+    loads[0].wait()
+    for f in range(3):
+        value = spread(lat[f].astype(F32))
+        values[0, 0, f] = fold(value * gain[0])
+        own_squares(f, value)
+    partial_a[0, 0] = squares[...].astype(BF16)
 
     sends = []
 
@@ -232,14 +230,19 @@
                 )
             )
 
+    def wait_values(j, slot):
+        remote(
+            values.at[j, 0], values.at[j, slot], value_send.at[j, slot], value_recv.at[j, slot], a_peer(j, slot)
+        ).wait_recv()
+
     def send_squares_b(j):
-        total = partial_a[j, 0]
+        total = partial_a[j, 0].astype(F32)
         for d in (1, 3, 2):
             remote(
                 partial_a.at[j, 0], partial_a.at[j, d], pa_send.at[j, d], pa_recv.at[j, d], b_peer(j, d)
             ).wait_recv()
-            total = total + partial_a[j, d]
-        partial_b[j, 0] = total
+            total = total + partial_a[j, d].astype(F32)
+        partial_b[j, 0] = total.astype(BF16)
         for d in far_first:
             start(
                 remote(
@@ -252,12 +255,38 @@
             )
 
     def scales(j):
-        total = partial_b[j, 0]
+        total = partial_b[j, 0].astype(F32)
         for d in (1, 3, 2):
             remote(
                 partial_b.at[j, 0], partial_b.at[j, d], pb_send.at[j, d], pb_recv.at[j, d], a_peer(j, d)
             ).wait_recv()
-            total = total + partial_b[j, d]
+            total = total + partial_b[j, d].astype(F32)
+        return lax.rsqrt(total / chans + 1e-06)
+
+    def any_copy(di, dj):
+        to = (SIDE - di) % SIDE * SIDE + (SIDE - dj) % SIDE
+        return remote(
+            partial_all.at[0],
+            partial_all.at[to],
+            all_send.at[di * SIDE + dj],
+            all_recv.at[to],
+            (t, SIDE * shifted(y, dj) + shifted(x, di)),
+        )
+
+    others = sorted(
+        [(di, dj) for di in range(SIDE) for dj in range(SIDE) if di or dj],
+        key=lambda o: -min(o[0], SIDE - o[0]) - min(o[1], SIDE - o[1]),
+    )
+
+    def send_squares_all():
+        for di, dj in others:
+            start(any_copy(di, dj))
+
+    def scales_all():
+        total = partial_all[0].astype(F32)
+        for di, dj in others[::-1]:
+            any_copy(SIDE - di if di else 0, SIDE - dj if dj else 0).wait_recv()
+            total = total + partial_all[di * SIDE + dj].astype(F32)
         return lax.rsqrt(total / chans + 1e-06)
 
     def turn_weights(j):
@@ -266,12 +295,12 @@
             part = weights[j, 9 * k : 9 * k + 9].astype(F32).reshape(9 * OWN, chans)
             part = jnp.concatenate([part, jnp.zeros((DEPTH - 9 * OWN, chans), F32)], axis=0)
             flat = jnp.transpose(part)
-            sums[0:chans, 0:DEPTH] = flat
+            turned[...] = flat
             for d in range(SIDE):
                 rows = []
                 for e in range(SIDE):
                     block = chan_at(j, shifted(index_a[j], d), shifted(index_b[j], e))
-                    rows.append(sums[pl.ds(pl.multiple_of(block * OWN, 8), OWN), 0:DEPTH])
+                    rows.append(turned[pl.ds(pl.multiple_of(block * OWN, 8), OWN), :])
                 rows = jnp.concatenate(rows, axis=0).astype(BF16)
                 if d == 0:
                     w_in[j, 0, k] = rows
@@ -290,24 +319,11 @@
                 )
             )
 
-    def send_gains(j):
-        for d in far_first:
-            start(
-                remote(
-                    gains.at[j, 0],
-                    gains.at[j, SIDE - d],
-                    gain_send.at[j, d],
-                    gain_recv.at[j, SIDE - d],
-                    a_peer(j, d),
-                )
-            )
-
     def stack_taps(slot, j, scale):
-        gain = tile4(gains[j, slot])
         for f in range(3):
             value = unfold(values[j, slot, f])
-            row = jnp.concatenate([scale[2 * f : 2 * f + 1], scale[2 * f + 1 : 2 * f + 2]], axis=1)
-            normed = value * row * gain
+            row = jnp.concatenate([scale[ROWS * f + r : ROWS * f + r + 1] for r in range(ROWS)], axis=1)
+            normed = value * row
             act = 0.5 * normed * (1.0 + jnp.tanh(0.5 * normed))
             act = act.astype(BF16).astype(F32)
             rows = [act[:, r * LANES : (r + 1) * LANES] for r in range(ROWS)]
@@ -325,29 +341,25 @@
             taps.append(jnp.zeros((DEPTH - 9 * OWN, WIDE), F32))
             stacked[f, slot] = jnp.concatenate(taps, axis=0).astype(BF16)
 
-    def convolve(j):
-        left = jnp.concatenate([w_in[j, s].reshape(3 * SIDE * OWN, DEPTH) for s in range(SIDE)], axis=1)
-        group = SIDE * OWN
-
-        def emit(frame, total):
-            for e in range(SIDE):
-                piece = total[e * OWN : (e + 1) * OWN]
-                if e == 0 and frame < 3:
-                    own_sums[frame] = piece
-                else:
-                    shares[j, e, frame] = fold(piece)
-
-        def product(f):
-            return jnp.dot(left, stacked[f].reshape(SIDE * DEPTH, WIDE), preferred_element_type=F32)
-
+    group = SIDE * OWN
+
+    def emit(j, frame, total):
+        for e in range(SIDE):
+            piece = total[e * OWN : (e + 1) * OWN]
+            if e == 0 and frame < 3:
+                own_sums[frame] = piece
+            else:
+                shares[j, e, frame] = fold(piece)
+
+    def emit_all(j, product):
         last = product(2)
-        emit(4, last[:group])
-        sums[0:group, :] = last[group : 2 * group]
-        sums[group : 2 * group, :] = last[2 * group :]
+        emit(j, 4, last[:group])
+        sums[2, :group] = last[group : 2 * group]
+        sums[2, group : 2 * group] = last[2 * group :]
         mid = product(1)
-        emit(3, sums[0:group, :] + mid[:group])
-        sums[group : 2 * group, :] += mid[group : 2 * group]
-        sums[0:group, :] = mid[2 * group :]
+        emit(j, 3, sums[2, :group] + mid[:group])
+        sums[2, group : 2 * group] += mid[group : 2 * group]
+        sums[2, :group] = mid[2 * group :]
 
         @pl.when(t < sections - 1)
         def _():
@@ -355,11 +367,39 @@
                 next_copy(j, e).start()
 
         first = product(0)
-        emit(2, sums[group : 2 * group, :] + first[:group])
-        emit(1, sums[0:group, :] + first[group : 2 * group])
-        emit(0, first[2 * group :])
+        emit(j, 2, sums[2, group : 2 * group] + first[:group])
+        emit(j, 1, sums[2, :group] + first[group : 2 * group])
+        emit(j, 0, first[2 * group :])
         for d in far_first:
             start(line_copy(j, d))
+
+    def left_of(j, slot):
+        return w_in[j, slot].reshape(3 * group, DEPTH)
+
+    def wait_weights(j, slot):
+        remote(
+            w_out.at[j, 0], w_in.at[j, slot], w_send.at[j, slot], w_recv.at[j, slot], a_peer(j, slot)
+        ).wait_recv()
+
+    def convolve_as_weights_come(j):
+        for slot in (0, 1, 3):
+            if slot:
+                wait_weights(j, slot)
+            for f in range(3):
+                part = jnp.dot(left_of(j, slot), stacked[f, slot], preferred_element_type=F32)
+                if slot:
+                    part = part + sums[f]
+                sums[f] = part
+        wait_weights(j, 2)
+        emit_all(j, lambda f: sums[f] + jnp.dot(left_of(j, 2), stacked[f, 2], preferred_element_type=F32))
+
+    def convolve(j):
+        for slot in (1, 3, 2):
+            wait_weights(j, slot)
+        left = jnp.concatenate([left_of(j, s) for s in range(SIDE)], axis=1)
+        emit_all(
+            j, lambda f: jnp.dot(left, stacked[f].reshape(SIDE * DEPTH, WIDE), preferred_element_type=F32)
+        )
 
     def next_copy(j, e):
         return remote(
@@ -414,54 +454,35 @@
     def _():
         from_before[...] = jnp.zeros(from_before.shape, BF16)
 
+    turn_weights(0)
+    pl.semaphore_wait(barrier, 2 * (SIDE - 1) + jnp.where(t < sections - 1, 2 * SIDE - 1, 0))
     send_squares_a(0)
     send_values(0)
-    send_gains(0)
-    send_gains(1)
-    turn_weights(0)
     send_weights(0)
     send_squares_b(0)
     turn_weights(1)
     scale = scales(0)
     for slot in (0, 1, 3, 2):
         if slot:
-            remote(
-                values.at[0, 0], values.at[0, slot], value_send.at[0, slot], value_recv.at[0, slot], a_peer(0, slot)
-            ).wait_recv()
-            remote(
-                gains.at[0, 0], gains.at[0, slot], gain_send.at[0, slot], gain_recv.at[0, slot], a_peer(0, slot)
-            ).wait_recv()
+            wait_values(0, slot)
         stack_taps(slot, 0, scale)
-    for slot in (1, 3, 2):
-        remote(
-            w_out.at[0, 0], w_in.at[0, slot], w_send.at[0, slot], w_recv.at[0, slot], a_peer(0, slot)
-        ).wait_recv()
+    convolve_as_weights_come(0)
     send_weights(1)
-    convolve(0)
 
     frames = collect(0)
     keep = tile4(lane_ids(OWN)) < COLS
     for f in range(3):
         middle = jnp.where(keep, frames[f], 0.0).astype(BF16).astype(F32)
-        values[1, 0, f] = fold(middle)
-        own_squares(1, f, middle)
-    send_squares_a(1)
+        values[1, 0, f] = fold(middle * gain[1])
+        own_squares(f, middle)
+    partial_all[0] = squares[...].astype(BF16)
+    send_squares_all()
     send_values(1)
-    send_squares_b(1)
-    scale = scales(1)
+    scale = scales_all()
     for slot in (0, 1, 3, 2):
         if slot:
-            remote(
-                gains.at[1, 0], gains.at[1, slot], gain_send.at[1, slot], gain_recv.at[1, slot], a_peer(1, slot)
-            ).wait_recv()
-            remote(
-                values.at[1, 0], values.at[1, slot], value_send.at[1, slot], value_recv.at[1, slot], a_peer(1, slot)
-            ).wait_recv()
+            wait_values(1, slot)
         stack_taps(slot, 1, scale)
-    for slot in (1, 3, 2):
-        remote(
-            w_out.at[1, 0], w_in.at[1, slot], w_send.at[1, slot], w_recv.at[1, slot], a_peer(1, slot)
-        ).wait_recv()
     convolve(1)
     frames = collect(1)
     for f in range(3):
@@ -481,7 +502,7 @@
     frames = latent.shape[1]
     chans = weight_one.shape[3]
     dma = pltpu.SemaphoreType.DMA
-    anywhere = pl.BlockSpec(memory_space=pl.ANY)
+    anywhere = pl.BlockSpec(memory_space=pltpu.HBM)
     result = pl.pallas_call(
         functools.partial(kernel, sections, chans),
         out_shape=jax.ShapeDtypeStruct((frames, OWN, ROWS * COLS), BF16),
@@ -492,23 +513,27 @@
             pltpu.VMEM((2, 27, OWN, chans), BF16),
             pltpu.VMEM((4, 1, OWN), F32),
             pltpu.VMEM((LANES, LANES), F32),
-            pltpu.VMEM((2, SIDE, OWN, LANES), F32),
             pltpu.VMEM((2, SIDE, frames, 2 * OWN, HALF), BF16),
-            pltpu.VMEM((2, SIDE, 8, HALF), F32),
-            pltpu.VMEM((2, SIDE, 8, HALF), F32),
+            pltpu.VMEM((16, LANES), F32),
+            pltpu.VMEM((1, SIDE, 16, LANES), BF16),
+            pltpu.VMEM((1, SIDE, 16, LANES), BF16),
+            pltpu.VMEM((SIDE * SIDE, 16, LANES), BF16),
+            pltpu.VMEM((chans, DEPTH), F32),
             pltpu.VMEM((2, SIDE - 1, 3, SIDE * OWN, DEPTH), BF16),
             pltpu.VMEM((2, SIDE, 3, SIDE * OWN, DEPTH), BF16),
             pltpu.VMEM((frames, SIDE, DEPTH, WIDE), BF16),
-            pltpu.VMEM((chans, WIDE), F32),
+            pltpu.VMEM((frames, 3 * SIDE * OWN, WIDE), F32),
             pltpu.VMEM((frames, OWN, WIDE), F32),
             pltpu.VMEM((2, SIDE, frames + 2, 2 * OWN, HALF), BF16),
             pltpu.VMEM((2, SIDE, frames, 2 * OWN, HALF), BF16),
             pltpu.VMEM((2, SIDE, 2, 2 * OWN, HALF), BF16),
             dma((7,)),
+            dma((SIDE * SIDE,)),
+            dma((SIDE * SIDE,)),
         ]
-        + [dma((2, SIDE))] * 14,
+        + [dma((2, SIDE))] * 12,
         compiler_params=pltpu.CompilerParams(
-            collective_id=0, has_side_effects=True, vmem_limit_bytes=40 * 1024 * 1024
+            collective_id=0, has_side_effects=True, vmem_limit_bytes=60 * 1024 * 1024
         ),
     )(
         jnp.transpose(latent, (1, 0, 2)),

time: 45.6 us -> 39.8 us (0.87)
  Pallas kernels: 41 us -> 38.1 us
  local copies, waits for them, and re-layouts: 4.27 us -> 1.52 us
    pallas_call x1, Pallas kernels: 41 us -> 38.1 us  [block(): pl.pallas_call(functools.partial(kernel, sections, chans), out_shape=jax....]
    unnamed x15 -> x1, local copies, waits for them, and re-layouts: 4.27 us -> 1.52 us
where the time goes in v2:
time: 39.8 us; the launch traced here: 39.6 us
  Pallas kernels  38.1 us (96%)
  local copies, waits for them, and re-layouts  1.52 us (4%)
    pallas_call x1, Pallas kernels, block(): pl.pallas_call(functools.partial(kernel, sections, chans), out_shape=jax....  38.1 us
    unnamed x1, local copies, waits for them, and re-layouts  1.52 us

profile of v2, /device:TPU:1, one launch (start us, length us, event | category | flops | bytes accessed | tf_op | source)
XLA Modules:
  0.0 39.6 jit_solution(9003322546343769584)
XLA Ops:
  0.0 38.1 %shard_map.73 = bf16[3,24,416]{2,1,0:T(8,128)(2,1)} custom-call(bf16[3,24,416]{2,1,0:T(8,128)(2,1)} %bitcast.11, bf16[27,24,384]{2,1,0:T(8,128)(2,1)} %bitcast.8, bf16[27,24,384]{2,1,0:T(8,128)(2,1)} %bitcast.9, f32[1,24]{1,0:T(1,128)} %bitcast.12, f32[1,24]{1,0:T(1,128)} %bitcast.13, f32[1,24]{1,0:T(1,128)} %bitcast.14, f32[1,24]{1,0:T(1,128)} %bitcast.15), custom_call_target="tpu_custom_call" | custom-call | tf_op jit(solution)/shard_map/pallas_call | solution.py:506
  38.1 1.5 %copy.9 = bf16[24,3,416]{2,0,1:T(8,128)(2,1)} copy(bf16[24,3,416]{2,0,1:T(8,128)(2,1)} %bitcast.10) | data formatting | bytes 119808

commit v3 on v2

--- a/solution.py
+++ b/solution.py
@@ -86,8 +86,6 @@
     flipped,
     values,
     squares,
-    partial_a,
-    partial_b,
     partial_all,
     turned,
     w_out,
@@ -103,16 +101,14 @@
     all_recv,
     value_send,
     value_recv,
-    pa_send,
-    pa_recv,
-    pb_send,
-    pb_recv,
     w_send,
     w_recv,
     line_send,
     line_recv,
     next_send,
     next_recv,
+    next_ready,
+    ready,
 ):
     t = lax.axis_index("tm")
     chan = lax.axis_index("chan")
@@ -146,7 +142,7 @@
             device_id_type=pl.DeviceIdType.MESH,
         )
 
-    far_first = (2, 1, 3)
+    near, far, far_first = (1, 3), (2,), (2, 1, 3)
 
     loads = [
         pltpu.make_async_copy(lat_hbm, lat, local_sem.at[0]),
@@ -160,19 +156,19 @@
 
     barrier = pltpu.get_barrier_semaphore()
 
+    def tell(semaphore, device):
+        pl.semaphore_signal(semaphore, inc=1, device_id=device, device_id_type=pl.DeviceIdType.MESH)
+
     def greet(device):
-        pl.semaphore_signal(barrier, inc=1, device_id=device, device_id_type=pl.DeviceIdType.MESH)
-
-    for d in range(1, SIDE):
+        tell(barrier, device)
+
+    for d in (1, 2, 3):
         greet((t, SIDE * y + shifted(x, d)))
         greet((t, SIDE * shifted(y, d) + x))
 
-    @pl.when(t > 0)
+    @pl.when(t < sections - 1)
     def _():
-        greet((t - 1, chan))
-        for d in range(1, SIDE):
-            greet((t - 1, SIDE * y + shifted(x, d)))
-            greet((t - 1, SIDE * shifted(y, d) + x))
+        greet((t + 1, chan))
 
     def own_squares(f, value):
         sums_of = jnp.sum(value * value, axis=0, keepdims=True)
@@ -198,7 +194,7 @@
         value = spread(lat[f].astype(F32))
         values[0, 0, f] = fold(value * gain[0])
         own_squares(f, value)
-    partial_a[0, 0] = squares[...].astype(BF16)
+    partial_all[0, 0] = squares[...].astype(BF16)
 
     sends = []
 
@@ -206,20 +202,8 @@
         copy.start()
         sends.append(copy)
 
-    def send_squares_a(j):
-        for d in far_first:
-            start(
-                remote(
-                    partial_a.at[j, 0],
-                    partial_a.at[j, SIDE - d],
-                    pa_send.at[j, d],
-                    pa_recv.at[j, SIDE - d],
-                    b_peer(j, d),
-                )
-            )
-
-    def send_values(j):
-        for d in far_first:
+    def send_values(j, steps):
+        for d in steps:
             start(
                 remote(
                     values.at[j, 0],
@@ -235,41 +219,13 @@
             values.at[j, 0], values.at[j, slot], value_send.at[j, slot], value_recv.at[j, slot], a_peer(j, slot)
         ).wait_recv()
 
-    def send_squares_b(j):
-        total = partial_a[j, 0].astype(F32)
-        for d in (1, 3, 2):
-            remote(
-                partial_a.at[j, 0], partial_a.at[j, d], pa_send.at[j, d], pa_recv.at[j, d], b_peer(j, d)
-            ).wait_recv()
-            total = total + partial_a[j, d].astype(F32)
-        partial_b[j, 0] = total.astype(BF16)
-        for d in far_first:
-            start(
-                remote(
-                    partial_b.at[j, 0],
-                    partial_b.at[j, SIDE - d],
-                    pb_send.at[j, d],
-                    pb_recv.at[j, SIDE - d],
-                    a_peer(j, d),
-                )
-            )
-
-    def scales(j):
-        total = partial_b[j, 0].astype(F32)
-        for d in (1, 3, 2):
-            remote(
-                partial_b.at[j, 0], partial_b.at[j, d], pb_send.at[j, d], pb_recv.at[j, d], a_peer(j, d)
-            ).wait_recv()
-            total = total + partial_b[j, d].astype(F32)
-        return lax.rsqrt(total / chans + 1e-06)
-
-    def any_copy(di, dj):
+    def any_copy(j, di, dj):
         to = (SIDE - di) % SIDE * SIDE + (SIDE - dj) % SIDE
         return remote(
-            partial_all.at[0],
-            partial_all.at[to],
-            all_send.at[di * SIDE + dj],
-            all_recv.at[to],
+            partial_all.at[j, 0],
+            partial_all.at[j, to],
+            all_send.at[j, di * SIDE + dj],
+            all_recv.at[j, to],
             (t, SIDE * shifted(y, dj) + shifted(x, di)),
         )
 
@@ -278,15 +234,15 @@
         key=lambda o: -min(o[0], SIDE - o[0]) - min(o[1], SIDE - o[1]),
     )
 
-    def send_squares_all():
+    def send_squares_all(j):
         for di, dj in others:
-            start(any_copy(di, dj))
-
-    def scales_all():
-        total = partial_all[0].astype(F32)
+            start(any_copy(j, di, dj))
+
+    def scales_all(j):
+        total = partial_all[j, 0].astype(F32)
         for di, dj in others[::-1]:
-            any_copy(SIDE - di if di else 0, SIDE - dj if dj else 0).wait_recv()
-            total = total + partial_all[di * SIDE + dj].astype(F32)
+            any_copy(j, SIDE - di if di else 0, SIDE - dj if dj else 0).wait_recv()
+            total = total + partial_all[j, di * SIDE + dj].astype(F32)
         return lax.rsqrt(total / chans + 1e-06)
 
     def turn_weights(j):
@@ -307,8 +263,8 @@
                 else:
                     w_out[j, d - 1, k] = rows
 
-    def send_weights(j):
-        for d in far_first:
+    def send_weights(j, steps):
+        for d in steps:
             start(
                 remote(
                     w_out.at[j, d - 1],
@@ -363,6 +319,8 @@
 
         @pl.when(t < sections - 1)
         def _():
+            if j == 0:
+                pl.semaphore_wait(next_ready, 1)
             for e in range(SIDE):
                 next_copy(j, e).start()
 
@@ -455,19 +413,27 @@
         from_before[...] = jnp.zeros(from_before.shape, BF16)
 
     turn_weights(0)
-    pl.semaphore_wait(barrier, 2 * (SIDE - 1) + jnp.where(t < sections - 1, 2 * SIDE - 1, 0))
-    send_squares_a(0)
-    send_values(0)
-    send_weights(0)
-    send_squares_b(0)
+    pl.semaphore_wait(barrier, 6 + jnp.where(t > 0, 1, 0))
+    for d in (1, 2, 3):
+        tell(ready, (t, SIDE * y + shifted(x, d)))
+    send_weights(0, near)
+    pl.semaphore_wait(ready, 3)
+    send_squares_all(0)
+    send_values(0, far_first)
+    send_weights(0, far)
+
+    @pl.when(t > 0)
+    def _():
+        tell(next_ready, (t - 1, chan))
+
     turn_weights(1)
-    scale = scales(0)
+    scale = scales_all(0)
     for slot in (0, 1, 3, 2):
         if slot:
             wait_values(0, slot)
         stack_taps(slot, 0, scale)
     convolve_as_weights_come(0)
-    send_weights(1)
+    send_weights(1, far_first)
 
     frames = collect(0)
     keep = tile4(lane_ids(OWN)) < COLS
@@ -475,10 +441,10 @@
         middle = jnp.where(keep, frames[f], 0.0).astype(BF16).astype(F32)
         values[1, 0, f] = fold(middle * gain[1])
         own_squares(f, middle)
-    partial_all[0] = squares[...].astype(BF16)
-    send_squares_all()
-    send_values(1)
-    scale = scales_all()
+    partial_all[1, 0] = squares[...].astype(BF16)
+    send_squares_all(1)
+    send_values(1, far_first)
+    scale = scales_all(1)
     for slot in (0, 1, 3, 2):
         if slot:
             wait_values(1, slot)
@@ -515,9 +481,7 @@
             pltpu.VMEM((LANES, LANES), F32),
             pltpu.VMEM((2, SIDE, frames, 2 * OWN, HALF), BF16),
             pltpu.VMEM((16, LANES), F32),
-            pltpu.VMEM((1, SIDE, 16, LANES), BF16),
-            pltpu.VMEM((1, SIDE, 16, LANES), BF16),
-            pltpu.VMEM((SIDE * SIDE, 16, LANES), BF16),
+            pltpu.VMEM((2, SIDE * SIDE, 16, LANES), BF16),
             pltpu.VMEM((chans, DEPTH), F32),
             pltpu.VMEM((2, SIDE - 1, 3, SIDE * OWN, DEPTH), BF16),
             pltpu.VMEM((2, SIDE, 3, SIDE * OWN, DEPTH), BF16),
@@ -528,14 +492,16 @@
             pltpu.VMEM((2, SIDE, frames, 2 * OWN, HALF), BF16),
             pltpu.VMEM((2, SIDE, 2, 2 * OWN, HALF), BF16),
             dma((7,)),
-            dma((SIDE * SIDE,)),
-            dma((SIDE * SIDE,)),
+            dma((2, SIDE * SIDE)),
+            dma((2, SIDE * SIDE)),
         ]
-        + [dma((2, SIDE))] * 12,
+        + [dma((2, SIDE))] * 8
+        + [pltpu.SemaphoreType.REGULAR] * 2,
         compiler_params=pltpu.CompilerParams(
-            collective_id=0, has_side_effects=True, vmem_limit_bytes=60 * 1024 * 1024
+            collective_id=0, has_side_effects=True, vmem_limit_bytes=40 * 1024 * 1024
         ),
     )(
+        *[pltpu.with_memory_space_constraint(v, pltpu.HBM) for v in (
         jnp.transpose(latent, (1, 0, 2)),
         weight_one.reshape(27, OWN, chans),
         weight_two.reshape(27, OWN, chans),
@@ -543,6 +509,7 @@
         bias_one.reshape(1, OWN),
         gain_two.reshape(1, OWN),
         bias_two.reshape(1, OWN),
+    )]
     )
     return jnp.transpose(result, (1, 0, 2))
 

time: 39.8 us -> 37.2 us (0.935)
  Pallas kernels: 38.1 us -> 36.3 us
  local copies, waits for them, and re-layouts: 1.52 us -> 0.64 us
    pallas_call x1, Pallas kernels: 38.1 us -> 36.3 us  [block(): pl.pallas_call(functools.partial(kernel, sections, chans), out_shape=jax....]
    unnamed x1, local copies, waits for them, and re-layouts: 1.52 us -> 0.64 us
where the time goes in v3:
time: 37.2 us; the launch traced here: 37 us
  Pallas kernels  36.3 us (98%)
  local copies, waits for them, and re-layouts  0.64 us (2%)
    pallas_call x1, Pallas kernels, block(): pl.pallas_call(functools.partial(kernel, sections, chans), out_shape=jax....  36.3 us

profile of v3, /device:TPU:1, one launch (start us, length us, event | category | flops | bytes accessed | tf_op | source)
XLA Modules:
  0.0 37.0 jit_solution(10332201227552294439)
XLA Ops:
  0.0 36.3 %shard_map.73 = bf16[3,24,416]{2,1,0:T(8,128)(2,1)S(1)} custom-call(bf16[3,24,416]{2,1,0:T(8,128)(2,1)} %bitcast.11, bf16[27,24,384]{2,1,0:T(8,128)(2,1)} %bitcast.9, bf16[27,24,384]{2,1,0:T(8,128)(2,1)} %bitcast.10, f32[1,24]{1,0:T(1,128)} %bitcast.12, f32[1,24]{1,0:T(1,128)} %bitcast.13, f32[1,24]{1,0:T(1,128)} %bitcast.14, f32[1,24]{1,0:T(1,128)} %bitcast.15), custom_call_target="tpu_custom_call" | custom-call | tf_op jit(solution)/shard_map/pallas_call | solution.py:472
  36.3 0.6 %copy.9 = bf16[24,3,416]{2,0,1:T(8,128)(2,1)} copy(bf16[24,3,416]{2,0,1:T(8,128)(2,1)S(1)} %bitcast.8) | data formatting | bytes 119808

commit v4 on v3

--- a/solution.py
+++ b/solution.py
@@ -13,7 +13,11 @@
 WIDE = ROWS * LANES
 SIDE = 4
 OWN = 24
-HALF = WIDE // 2
+FRAMES = 3
+MAIN = 384
+REST = ROWS * COLS - MAIN
+PACKED = FRAMES * MAIN + LANES
+PACKED_NEXT = 2 * MAIN + LANES
 DEPTH = 256
 F32 = jnp.float32
 BF16 = jnp.bfloat16
@@ -25,48 +29,84 @@
 
 
 def fold(value):
-    return jnp.concatenate([value[:, :HALF], value[:, HALF:]], axis=0).astype(BF16)
-
-
-def tile4(value):
-    return jnp.concatenate([value] * ROWS, axis=1)
+    half = PACKED // 2
+    return jnp.concatenate([value[:, :half], value[:, half:]], axis=0).astype(BF16)
+
+
+NEXT_HALF = (OWN // 8 * PACKED_NEXT + LANES) // 2
+
+
+def fold_next(value):
+    parts = [value[8 * n : 8 * n + 8] for n in range(OWN // 8)] + [jnp.zeros((8, LANES), F32)]
+    flat = jnp.concatenate(parts, axis=1)
+    return jnp.concatenate([flat[:, :NEXT_HALF], flat[:, NEXT_HALF:]], axis=0).astype(BF16)
+
+
+def unfold_next(value):
+    value = value.astype(F32)
+    flat = jnp.concatenate([value[:8], value[8:]], axis=1)
+    return jnp.concatenate(
+        [flat[:, PACKED_NEXT * n : PACKED_NEXT * (n + 1)] for n in range(OWN // 8)], axis=0
+    )
+
+
+def spread_lanes(value):
+    return jnp.concatenate([value] * (PACKED // LANES), axis=1)
 
 
 def lane_ids(rows):
     return lax.broadcasted_iota(jnp.int32, (rows, LANES), 1)
 
 
-def spread(frame):
-    flat = jnp.concatenate([frame, jnp.zeros((OWN, WIDE - ROWS * COLS), F32)], axis=1)
+def tiles(value):
+    return [value[:, n : n + LANES] for n in range(0, value.shape[1], LANES)]
+
+
+def spread(packed, f):
+    parts = tiles(packed)
+    cells = parts[3 * f : 3 * f + 3] + [pltpu.roll(parts[-1], LANES - REST * f, 1) if f else parts[-1]]
     lane = lane_ids(OWN)
     rows = []
     for row in range(ROWS):
         at, off = divmod(row * COLS, LANES)
-        piece = flat[:, at * LANES : (at + 1) * LANES]
+        piece = cells[at]
         if off:
-            after = flat[:, (at + 1) * LANES : (at + 2) * LANES]
             piece = jnp.where(
                 lane < LANES - off,
                 pltpu.roll(piece, LANES - off, 1),
-                pltpu.roll(after, LANES - off, 1),
+                pltpu.roll(cells[at + 1], LANES - off, 1),
             )
         rows.append(jnp.where(lane < COLS, piece, 0.0))
-    return jnp.concatenate(rows, axis=1)
-
-
-def squeeze(frame):
-    lane = lane_ids(OWN)
-    rows = [frame[:, r * LANES : (r + 1) * LANES] for r in range(ROWS)]
+    return rows
+
+
+def pack(frame, place):
+    rows = tiles(frame)
+    lane = lane_ids(frame.shape[0])
     pieces = []
-    for at in range(ROWS):
+    for at in range(MAIN // LANES):
         row, off = divmod(at * LANES, COLS)
-        piece = rows[row]
-        if off:
-            piece = pltpu.roll(piece, LANES - off, 1)
-        if row + 1 < ROWS:
-            piece = jnp.where(lane < COLS - off, piece, pltpu.roll(rows[row + 1], COLS - off, 1))
-        pieces.append(piece)
-    return jnp.concatenate(pieces, axis=1)[:, : ROWS * COLS]
+        piece = pltpu.roll(rows[row], LANES - off, 1) if off else rows[row]
+        pieces.append(jnp.where(lane < COLS - off, piece, pltpu.roll(rows[row + 1], COLS - off, 1)))
+    row, off = divmod(MAIN, COLS)
+    return jnp.concatenate(pieces, axis=1), pltpu.roll(rows[row], (LANES - off + REST * place) % LANES, 1)
+
+
+def join(packs):
+    lane = lane_ids(packs[0][0].shape[0])
+    rest = jnp.zeros(packs[0][1].shape, F32)
+    for place in range(len(packs) - 1, -1, -1):
+        rest = jnp.where(lane < REST * (place + 1), packs[place][1], rest)
+    return jnp.concatenate([main for main, _ in packs] + [rest], axis=1)
+
+
+def pack_latent(lat):
+    packs = []
+    for f in range(FRAMES):
+        frame = lat[f].astype(F32)
+        rest = jnp.concatenate([frame[:, MAIN:], jnp.zeros((OWN, LANES - REST), F32)], axis=1)
+        packs.append((frame[:, :MAIN], pltpu.roll(rest, REST * f, 1) if f else rest))
+    return join(packs)
 
 
 def kernel(
@@ -94,6 +134,7 @@
     sums,
     own_sums,
     shares,
+    shares_next,
     from_line,
     from_before,
     local_sem,
@@ -170,10 +211,10 @@
     def _():
         greet((t + 1, chan))
 
-    def own_squares(f, value):
+    def own_squares(value):
         sums_of = jnp.sum(value * value, axis=0, keepdims=True)
-        for r in range(ROWS):
-            squares[ROWS * f + r : ROWS * f + r + 1, :] = sums_of[:, r * LANES : (r + 1) * LANES]
+        for n, part in enumerate(tiles(sums_of)):
+            squares[n : n + 1, :] = part
 
     for n in range(4):
         loads[3 + n].wait()
@@ -186,14 +227,13 @@
         return jnp.broadcast_to(columns[:, n : n + 1], (OWN, LANES))
 
     bias = [column(1), column(3)]
-    gain = [tile4(column(0)), tile4(column(2))]
+    gain = [spread_lanes(column(0)), spread_lanes(column(2))]
 
     squares[...] = jnp.zeros((16, LANES), F32)
     loads[0].wait()
-    for f in range(3):
-        value = spread(lat[f].astype(F32))
-        values[0, 0, f] = fold(value * gain[0])
-        own_squares(f, value)
+    value = pack_latent(lat)
+    values[0, 0] = fold(value * gain[0])
+    own_squares(value)
     partial_all[0, 0] = squares[...].astype(BF16)
 
     sends = []
@@ -276,13 +316,11 @@
             )
 
     def stack_taps(slot, j, scale):
-        for f in range(3):
-            value = unfold(values[j, slot, f])
-            row = jnp.concatenate([scale[ROWS * f + r : ROWS * f + r + 1] for r in range(ROWS)], axis=1)
-            normed = value * row
-            act = 0.5 * normed * (1.0 + jnp.tanh(0.5 * normed))
-            act = act.astype(BF16).astype(F32)
-            rows = [act[:, r * LANES : (r + 1) * LANES] for r in range(ROWS)]
+        normed = unfold(values[j, slot]) * jnp.concatenate([scale[n : n + 1] for n in range(PACKED // LANES)], axis=1)
+        act = 0.5 * normed * (1.0 + jnp.tanh(0.5 * normed))
+        act = act.astype(BF16).astype(F32)
+        for f in range(FRAMES):
+            rows = spread(act, f)
             shifts = [
                 [pltpu.roll(r, 1, 1) for r in rows],
                 rows,
@@ -299,21 +337,15 @@
 
     group = SIDE * OWN
 
-    def emit(j, frame, total):
-        for e in range(SIDE):
-            piece = total[e * OWN : (e + 1) * OWN]
-            if e == 0 and frame < 3:
-                own_sums[frame] = piece
-            else:
-                shares[j, e, frame] = fold(piece)
-
     def emit_all(j, product):
         last = product(2)
-        emit(j, 4, last[:group])
+        later = pack(last[:group], 1)
         sums[2, :group] = last[group : 2 * group]
         sums[2, group : 2 * group] = last[2 * group :]
         mid = product(1)
-        emit(j, 3, sums[2, :group] + mid[:group])
+        later = join([pack(sums[2, :group] + mid[:group], 0), later])
+        for e in range(SIDE):
+            shares_next[j, e] = fold_next(later[e * OWN : (e + 1) * OWN])
         sums[2, group : 2 * group] += mid[group : 2 * group]
         sums[2, :group] = mid[2 * group :]
 
@@ -325,9 +357,15 @@
                 next_copy(j, e).start()
 
         first = product(0)
-        emit(j, 2, sums[2, group : 2 * group] + first[:group])
-        emit(j, 1, sums[2, :group] + first[group : 2 * group])
-        emit(j, 0, first[2 * group :])
+        frames = [
+            first[2 * group :],
+            sums[2, :group] + first[group : 2 * group],
+            sums[2, group : 2 * group] + first[:group],
+        ]
+        packed = join([pack(frame, f) for f, frame in enumerate(frames)])
+        own_sums[...] = packed[:OWN]
+        for e in range(1, SIDE):
+            shares[j, e] = fold(packed[e * OWN : (e + 1) * OWN])
         for d in far_first:
             start(line_copy(j, d))
 
@@ -361,7 +399,7 @@
 
     def next_copy(j, e):
         return remote(
-            shares.at[j, e, pl.ds(3, 2)],
+            shares_next.at[j, e],
             from_before.at[j, e],
             next_send.at[j, e],
             next_recv.at[j, e],
@@ -370,7 +408,7 @@
 
     def line_copy(j, d):
         return remote(
-            shares.at[j, d, pl.ds(0, 3)],
+            shares.at[j, d],
             from_line.at[j, SIDE - d],
             line_send.at[j, d],
             line_recv.at[j, SIDE - d],
@@ -397,16 +435,20 @@
                 line_recv.at[j, d],
                 b_peer(j, d),
             ).wait_recv()
-        frames = []
-        for f in range(3):
-            total = own_sums[f] + tile4(bias[j])
-            for d in range(1, SIDE):
-                total = total + unfold(from_line[j, d, f])
-            if f < 2:
-                for e in range(SIDE):
-                    total = total + unfold(from_before[j, e, f])
-            frames.append(total)
-        return frames
+        total = own_sums[...] + spread_lanes(bias[j])
+        for d in range(1, SIDE):
+            total = total + unfold(from_line[j, d])
+        before = unfold_next(from_before[j, 0])
+        for e in range(1, SIDE):
+            before = before + unfold_next(from_before[j, e])
+        return jnp.concatenate(
+            [
+                total[:, : 2 * MAIN] + before[:, : 2 * MAIN],
+                total[:, 2 * MAIN : 3 * MAIN],
+                total[:, 3 * MAIN :] + before[:, 2 * MAIN :],
+            ],
+            axis=1,
+        )
 
     @pl.when(t == 0)
     def _():
@@ -435,12 +477,11 @@
     convolve_as_weights_come(0)
     send_weights(1, far_first)
 
-    frames = collect(0)
-    keep = tile4(lane_ids(OWN)) < COLS
-    for f in range(3):
-        middle = jnp.where(keep, frames[f], 0.0).astype(BF16).astype(F32)
-        values[1, 0, f] = fold(middle * gain[1])
-        own_squares(f, middle)
+    middle = collect(0)
+    rest = jnp.where(lane_ids(OWN) < FRAMES * REST, middle[:, FRAMES * MAIN :], 0.0)
+    middle = jnp.concatenate([middle[:, : FRAMES * MAIN], rest], axis=1).astype(BF16).astype(F32)
+    values[1, 0] = fold(middle * gain[1])
+    own_squares(middle)
     partial_all[1, 0] = squares[...].astype(BF16)
     send_squares_all(1)
     send_values(1, far_first)
@@ -450,9 +491,12 @@
             wait_values(1, slot)
         stack_taps(slot, 1, scale)
     convolve(1)
-    frames = collect(1)
-    for f in range(3):
-        out_ref[f] = (lat[f].astype(F32) + squeeze(frames[f])).astype(BF16)
+    result = pack_latent(lat) + collect(1)
+    for f in range(FRAMES):
+        rest = result[:, FRAMES * MAIN :]
+        rest = pltpu.roll(rest, LANES - REST * f, 1) if f else rest
+        frame = jnp.concatenate([result[:, f * MAIN : (f + 1) * MAIN], rest], axis=1)
+        out_ref[f] = frame[:, : ROWS * COLS].astype(BF16)
 
     for copy in sends:
         copy.wait_send()
@@ -479,7 +523,7 @@
             pltpu.VMEM((2, 27, OWN, chans), BF16),
             pltpu.VMEM((4, 1, OWN), F32),
             pltpu.VMEM((LANES, LANES), F32),
-            pltpu.VMEM((2, SIDE, frames, 2 * OWN, HALF), BF16),
+            pltpu.VMEM((2, SIDE, 2 * OWN, PACKED // 2), BF16),
             pltpu.VMEM((16, LANES), F32),
             pltpu.VMEM((2, SIDE * SIDE, 16, LANES), BF16),
             pltpu.VMEM((chans, DEPTH), F32),
@@ -487,10 +531,11 @@
             pltpu.VMEM((2, SIDE, 3, SIDE * OWN, DEPTH), BF16),
             pltpu.VMEM((frames, SIDE, DEPTH, WIDE), BF16),
             pltpu.VMEM((frames, 3 * SIDE * OWN, WIDE), F32),
-            pltpu.VMEM((frames, OWN, WIDE), F32),
-            pltpu.VMEM((2, SIDE, frames + 2, 2 * OWN, HALF), BF16),
-            pltpu.VMEM((2, SIDE, frames, 2 * OWN, HALF), BF16),
-            pltpu.VMEM((2, SIDE, 2, 2 * OWN, HALF), BF16),
+            pltpu.VMEM((OWN, PACKED), F32),
+            pltpu.VMEM((2, SIDE, 2 * OWN, PACKED // 2), BF16),
+            pltpu.VMEM((2, SIDE, 16, NEXT_HALF), BF16),
+            pltpu.VMEM((2, SIDE, 2 * OWN, PACKED // 2), BF16),
+            pltpu.VMEM((2, SIDE, 16, NEXT_HALF), BF16),
             dma((7,)),
             dma((2, SIDE * SIDE)),
             dma((2, SIDE * SIDE)),

time: 37.2 us -> 37.2 us (level)
  no operation moved by 1% of the time
where the time goes in v4:
time: 37.2 us; the launch traced here: 37.1 us
  Pallas kernels  36.5 us (98%)
  local copies, waits for them, and re-layouts  0.64 us (2%)
    pallas_call x1, Pallas kernels, block(): pl.pallas_call(functools.partial(kernel, sections, chans), out_shape=jax....  36.5 us

profile of v4, /device:TPU:1, one launch (start us, length us, event | category | flops | bytes accessed | tf_op | source)
XLA Modules:
  0.0 37.1 jit_solution(9146314189692603262)
XLA Ops:
  0.0 36.5 %shard_map.73 = bf16[3,24,416]{2,1,0:T(8,128)(2,1)S(1)} custom-call(bf16[3,24,416]{2,1,0:T(8,128)(2,1)} %bitcast.11, bf16[27,24,384]{2,1,0:T(8,128)(2,1)} %bitcast.9, bf16[27,24,384]{2,1,0:T(8,128)(2,1)} %bitcast.10, f32[1,24]{1,0:T(1,128)} %bitcast.12, f32[1,24]{1,0:T(1,128)} %bitcast.13, f32[1,24]{1,0:T(1,128)} %bitcast.14, f32[1,24]{1,0:T(1,128)} %bitcast.15), custom_call_target="tpu_custom_call" | custom-call | tf_op jit(solution)/shard_map/pallas_call | solution.py:516
  36.5 0.6 %copy.9 = bf16[24,3,416]{2,0,1:T(8,128)(2,1)} copy(bf16[24,3,416]{2,0,1:T(8,128)(2,1)S(1)} %bitcast.8) | data formatting | bytes 119808

commit v5 on v4

--- a/solution.py
+++ b/solution.py
@@ -274,9 +274,10 @@
         key=lambda o: -min(o[0], SIDE - o[0]) - min(o[1], SIDE - o[1]),
     )
 
-    def send_squares_all(j):
+    def send_squares(j, diagonal):
         for di, dj in others:
-            start(any_copy(j, di, dj))
+            if bool(di and dj) == diagonal:
+                start(any_copy(j, di, dj))
 
     def scales_all(j):
         total = partial_all[j, 0].astype(F32)
@@ -458,11 +459,12 @@
     pl.semaphore_wait(barrier, 6 + jnp.where(t > 0, 1, 0))
     for d in (1, 2, 3):
         tell(ready, (t, SIDE * y + shifted(x, d)))
-    send_weights(0, near)
-    pl.semaphore_wait(ready, 3)
-    send_squares_all(0)
+    send_squares(0, False)
     send_values(0, far_first)
     send_weights(0, far)
+    pl.semaphore_wait(ready, 3)
+    send_squares(0, True)
+    send_weights(0, near)
 
     @pl.when(t > 0)
     def _():
@@ -483,7 +485,8 @@
     values[1, 0] = fold(middle * gain[1])
     own_squares(middle)
     partial_all[1, 0] = squares[...].astype(BF16)
-    send_squares_all(1)
+    send_squares(1, True)
+    send_squares(1, False)
     send_values(1, far_first)
     scale = scales_all(1)
     for slot in (0, 1, 3, 2):

time: 37.2 us -> 36.6 us (0.984)
  Pallas kernels: 36.5 us -> 35.8 us
    pallas_call x1, Pallas kernels: 36.5 us -> 35.8 us  [block(): pl.pallas_call(functools.partial(kernel, sections, chans), out_shape=jax....]
where the time goes in v5:
time: 36.6 us; the launch traced here: 36.5 us
  Pallas kernels  35.8 us (98%)
  local copies, waits for them, and re-layouts  0.64 us (2%)
    pallas_call x1, Pallas kernels, block(): pl.pallas_call(functools.partial(kernel, sections, chans), out_shape=jax....  35.8 us

profile of v5, /device:TPU:1, one launch (start us, length us, event | category | flops | bytes accessed | tf_op | source)
XLA Modules:
  0.0 36.5 jit_solution(11022717239978960961)
XLA Ops:
  0.0 35.8 %shard_map.73 = bf16[3,24,416]{2,1,0:T(8,128)(2,1)S(1)} custom-call(bf16[3,24,416]{2,1,0:T(8,128)(2,1)} %bitcast.11, bf16[27,24,384]{2,1,0:T(8,128)(2,1)} %bitcast.9, bf16[27,24,384]{2,1,0:T(8,128)(2,1)} %bitcast.10, f32[1,24]{1,0:T(1,128)} %bitcast.12, f32[1,24]{1,0:T(1,128)} %bitcast.13, f32[1,24]{1,0:T(1,128)} %bitcast.14, f32[1,24]{1,0:T(1,128)} %bitcast.15), custom_call_target="tpu_custom_call" | custom-call | tf_op jit(solution)/shard_map/pallas_call | solution.py:519
  35.8 0.6 %copy.9 = bf16[24,3,416]{2,0,1:T(8,128)(2,1)} copy(bf16[24,3,416]{2,0,1:T(8,128)(2,1)S(1)} %bitcast.8) | data formatting | bytes 119808

commit v6 on v5

--- a/solution.py
+++ b/solution.py
@@ -17,7 +17,6 @@
 MAIN = 384
 REST = ROWS * COLS - MAIN
 PACKED = FRAMES * MAIN + LANES
-PACKED_NEXT = 2 * MAIN + LANES
 DEPTH = 256
 F32 = jnp.float32
 BF16 = jnp.bfloat16
@@ -33,21 +32,24 @@
     return jnp.concatenate([value[:, :half], value[:, half:]], axis=0).astype(BF16)
 
 
-NEXT_HALF = (OWN // 8 * PACKED_NEXT + LANES) // 2
+def flat_half(width):
+    return (OWN // 8 * width + LANES) // (2 * LANES) * LANES
 
 
 def fold_next(value):
-    parts = [value[8 * n : 8 * n + 8] for n in range(OWN // 8)] + [jnp.zeros((8, LANES), F32)]
+    width = value.shape[1]
+    half = flat_half(width)
+    parts = [value[8 * n : 8 * n + 8] for n in range(OWN // 8)]
+    if 2 * half > OWN // 8 * width:
+        parts.append(jnp.zeros((8, LANES), F32))
     flat = jnp.concatenate(parts, axis=1)
-    return jnp.concatenate([flat[:, :NEXT_HALF], flat[:, NEXT_HALF:]], axis=0).astype(BF16)
-
-
-def unfold_next(value):
+    return jnp.concatenate([flat[:, :half], flat[:, half:]], axis=0).astype(BF16)
+
+
+def unfold_next(value, width):
     value = value.astype(F32)
     flat = jnp.concatenate([value[:8], value[8:]], axis=1)
-    return jnp.concatenate(
-        [flat[:, PACKED_NEXT * n : PACKED_NEXT * (n + 1)] for n in range(OWN // 8)], axis=0
-    )
+    return jnp.concatenate([flat[:, width * n : width * (n + 1)] for n in range(OWN // 8)], axis=0)
 
 
 def spread_lanes(value):
@@ -134,9 +136,11 @@
     sums,
     own_sums,
     shares,
-    shares_next,
+    shares_far,
+    shares_near,
     from_line,
-    from_before,
+    before_far,
+    before_near,
     local_sem,
     all_send,
     all_recv,
@@ -183,7 +187,7 @@
             device_id_type=pl.DeviceIdType.MESH,
         )
 
-    near, far, far_first = (1, 3), (2,), (2, 1, 3)
+    near, far, far_first, next_order = (1, 3), (2,), (2, 1, 3), (2, 1, 3, 0)
 
     loads = [
         pltpu.make_async_copy(lat_hbm, lat, local_sem.at[0]),
@@ -340,23 +344,34 @@
 
     def emit_all(j, product):
         last = product(2)
-        later = pack(last[:group], 1)
-        sums[2, :group] = last[group : 2 * group]
-        sums[2, group : 2 * group] = last[2 * group :]
-        mid = product(1)
-        later = join([pack(sums[2, :group] + mid[:group], 0), later])
+        main, rest = pack(last[:group], 1)
         for e in range(SIDE):
-            shares_next[j, e] = fold_next(later[e * OWN : (e + 1) * OWN])
-        sums[2, group : 2 * group] += mid[group : 2 * group]
-        sums[2, :group] = mid[2 * group :]
+            shares_far[j, e] = fold_next(main[e * OWN : (e + 1) * OWN])
 
         @pl.when(t < sections - 1)
         def _():
             if j == 0:
                 pl.semaphore_wait(next_ready, 1)
-            for e in range(SIDE):
-                next_copy(j, e).start()
-
+            for e in next_order:
+                next_copy(j, e, 0).start()
+
+        sums[2, :group] = last[group : 2 * group]
+        sums[2, group : 2 * group] = last[2 * group :]
+        mid = product(1)
+        nearer, its_rest = pack(sums[2, :group] + mid[:group], 0)
+        lane = lane_ids(group)
+        rest = jnp.where(lane < REST, its_rest, jnp.where(lane < 2 * REST, rest, 0.0))
+        nearer = jnp.concatenate([nearer, rest], axis=1)
+        for e in range(SIDE):
+            shares_near[j, e] = fold_next(nearer[e * OWN : (e + 1) * OWN])
+
+        @pl.when(t < sections - 1)
+        def _():
+            for e in next_order:
+                next_copy(j, e, 1).start()
+
+        sums[2, group : 2 * group] += mid[group : 2 * group]
+        sums[2, :group] = mid[2 * group :]
         first = product(0)
         frames = [
             first[2 * group :],
@@ -398,12 +413,12 @@
             j, lambda f: jnp.dot(left, stacked[f].reshape(SIDE * DEPTH, WIDE), preferred_element_type=F32)
         )
 
-    def next_copy(j, e):
+    def next_copy(j, e, part):
         return remote(
-            shares_next.at[j, e],
-            from_before.at[j, e],
-            next_send.at[j, e],
-            next_recv.at[j, e],
+            (shares_far, shares_near)[part].at[j, e],
+            (before_far, before_near)[part].at[j, e],
+            next_send.at[j, part, e],
+            next_recv.at[j, part, e],
             b_peer(j, e, 1),
         )
 
@@ -419,14 +434,15 @@
     def collect(j):
         @pl.when(t > 0)
         def _():
-            for e in range(SIDE):
-                remote(
-                    from_before.at[j, e],
-                    from_before.at[j, e],
-                    next_send.at[j, e],
-                    next_recv.at[j, e],
-                    (t, chan_at(j, shifted(index_a[j], 1), index_b[j])),
-                ).wait_recv()
+            for part, landed in enumerate((before_far, before_near)):
+                for e in range(SIDE):
+                    remote(
+                        landed.at[j, e],
+                        landed.at[j, e],
+                        next_send.at[j, part, e],
+                        next_recv.at[j, part, e],
+                        (t, chan_at(j, shifted(index_a[j], 1), index_b[j])),
+                    ).wait_recv()
 
         for d in (1, 3, 2):
             remote(
@@ -439,21 +455,25 @@
         total = own_sums[...] + spread_lanes(bias[j])
         for d in range(1, SIDE):
             total = total + unfold(from_line[j, d])
-        before = unfold_next(from_before[j, 0])
+        second = unfold_next(before_far[j, 0], MAIN)
+        first = unfold_next(before_near[j, 0], MAIN + LANES)
         for e in range(1, SIDE):
-            before = before + unfold_next(from_before[j, e])
+            second = second + unfold_next(before_far[j, e], MAIN)
+            first = first + unfold_next(before_near[j, e], MAIN + LANES)
         return jnp.concatenate(
             [
-                total[:, : 2 * MAIN] + before[:, : 2 * MAIN],
+                total[:, :MAIN] + first[:, :MAIN],
+                total[:, MAIN : 2 * MAIN] + second,
                 total[:, 2 * MAIN : 3 * MAIN],
-                total[:, 3 * MAIN :] + before[:, 2 * MAIN :],
+                total[:, 3 * MAIN :] + first[:, MAIN:],
             ],
             axis=1,
         )
 
     @pl.when(t == 0)
     def _():
-        from_before[...] = jnp.zeros(from_before.shape, BF16)
+        before_far[...] = jnp.zeros(before_far.shape, BF16)
+        before_near[...] = jnp.zeros(before_near.shape, BF16)
 
     turn_weights(0)
     pl.semaphore_wait(barrier, 6 + jnp.where(t > 0, 1, 0))
@@ -508,7 +528,8 @@
     def _():
         for j in range(2):
             for e in range(SIDE):
-                next_copy(j, e).wait_send()
+                for part in range(2):
+                    next_copy(j, e, part).wait_send()
 
 
 def block(sections, latent, gain_one, weight_one, bias_one, gain_two, weight_two, bias_two):
@@ -536,14 +557,17 @@
             pltpu.VMEM((frames, 3 * SIDE * OWN, WIDE), F32),
             pltpu.VMEM((OWN, PACKED), F32),
             pltpu.VMEM((2, SIDE, 2 * OWN, PACKED // 2), BF16),
-            pltpu.VMEM((2, SIDE, 16, NEXT_HALF), BF16),
+            pltpu.VMEM((2, SIDE, 16, flat_half(MAIN)), BF16),
+            pltpu.VMEM((2, SIDE, 16, flat_half(MAIN + LANES)), BF16),
             pltpu.VMEM((2, SIDE, 2 * OWN, PACKED // 2), BF16),
-            pltpu.VMEM((2, SIDE, 16, NEXT_HALF), BF16),
+            pltpu.VMEM((2, SIDE, 16, flat_half(MAIN)), BF16),
+            pltpu.VMEM((2, SIDE, 16, flat_half(MAIN + LANES)), BF16),
             dma((7,)),
             dma((2, SIDE * SIDE)),
             dma((2, SIDE * SIDE)),
         ]
-        + [dma((2, SIDE))] * 8
+        + [dma((2, SIDE))] * 6
+        + [dma((2, 2, SIDE))] * 2
         + [pltpu.SemaphoreType.REGULAR] * 2,
         compiler_params=pltpu.CompilerParams(
             collective_id=0, has_side_effects=True, vmem_limit_bytes=40 * 1024 * 1024

time: 36.6 us -> 36.1 us (0.986)
  Pallas kernels: 35.8 us -> 35.3 us
    pallas_call x1, Pallas kernels: 35.8 us -> 35.3 us  [block(): pl.pallas_call(functools.partial(kernel, sections, chans), out_shape=jax....]
where the time goes in v6:
time: 36.1 us; the launch traced here: 36 us
  Pallas kernels  35.3 us (98%)
  local copies, waits for them, and re-layouts  0.64 us (2%)
    pallas_call x1, Pallas kernels, block(): pl.pallas_call(functools.partial(kernel, sections, chans), out_shape=jax....  35.3 us

profile of v6, /device:TPU:1, one launch (start us, length us, event | category | flops | bytes accessed | tf_op | source)
XLA Modules:
  0.0 36.0 jit_solution(14837550259005288916)
XLA Ops:
  0.0 35.3 %shard_map.73 = bf16[3,24,416]{2,1,0:T(8,128)(2,1)S(1)} custom-call(bf16[3,24,416]{2,1,0:T(8,128)(2,1)} %bitcast.11, bf16[27,24,384]{2,1,0:T(8,128)(2,1)} %bitcast.9, bf16[27,24,384]{2,1,0:T(8,128)(2,1)} %bitcast.10, f32[1,24]{1,0:T(1,128)} %bitcast.12, f32[1,24]{1,0:T(1,128)} %bitcast.13, f32[1,24]{1,0:T(1,128)} %bitcast.14, f32[1,24]{1,0:T(1,128)} %bitcast.15), custom_call_target="tpu_custom_call" | custom-call | tf_op jit(solution)/shard_map/pallas_call | solution.py:540
  35.4 0.6 %copy.9 = bf16[24,3,416]{2,0,1:T(8,128)(2,1)} copy(bf16[24,3,416]{2,0,1:T(8,128)(2,1)S(1)} %bitcast.8) | data formatting | bytes 119808

commit v7 on v6

--- a/solution.py
+++ b/solution.py
@@ -196,8 +196,6 @@
     ]
     for n, ref in enumerate((g1_hbm, b1_hbm, g2_hbm, b2_hbm)):
         loads.append(pltpu.make_async_copy(ref, vecs.at[n], local_sem.at[3 + n]))
-    for load in loads:
-        load.start()
 
     barrier = pltpu.get_barrier_semaphore()
 
@@ -207,13 +205,16 @@
     def greet(device):
         tell(barrier, device)
 
-    for d in (1, 2, 3):
+    for d in far_first:
         greet((t, SIDE * y + shifted(x, d)))
         greet((t, SIDE * shifted(y, d) + x))
 
     @pl.when(t < sections - 1)
     def _():
         greet((t + 1, chan))
+
+    for load in loads:
+        load.start()
 
     def own_squares(value):
         sums_of = jnp.sum(value * value, axis=0, keepdims=True)
@@ -245,6 +246,18 @@
     def start(copy):
         copy.start()
         sends.append(copy)
+
+    def drain():
+        for copy in sends:
+            copy.wait_send()
+        sends.clear()
+
+    def drain_next(j):
+        @pl.when(t < sections - 1)
+        def _():
+            for e in range(SIDE):
+                for part in range(2):
+                    next_copy(j, e, part).wait_send()
 
     def send_values(j, steps):
         for d in steps:
@@ -394,7 +407,7 @@
         ).wait_recv()
 
     def convolve_as_weights_come(j):
-        for slot in (0, 1, 3):
+        for slot in (0, 2, 3):
             if slot:
                 wait_weights(j, slot)
             for f in range(3):
@@ -402,8 +415,8 @@
                 if slot:
                     part = part + sums[f]
                 sums[f] = part
-        wait_weights(j, 2)
-        emit_all(j, lambda f: sums[f] + jnp.dot(left_of(j, 2), stacked[f, 2], preferred_element_type=F32))
+        wait_weights(j, 1)
+        emit_all(j, lambda f: sums[f] + jnp.dot(left_of(j, 1), stacked[f, 1], preferred_element_type=F32))
 
     def convolve(j):
         for slot in (1, 3, 2):
@@ -496,6 +509,8 @@
         if slot:
             wait_values(0, slot)
         stack_taps(slot, 0, scale)
+    early = list(sends)
+    sends.clear()
     convolve_as_weights_come(0)
     send_weights(1, far_first)
 
@@ -505,15 +520,22 @@
     values[1, 0] = fold(middle * gain[1])
     own_squares(middle)
     partial_all[1, 0] = squares[...].astype(BF16)
+    send_squares(1, False)
     send_squares(1, True)
-    send_squares(1, False)
     send_values(1, far_first)
+    for copy in early:
+        copy.wait_send()
     scale = scales_all(1)
     for slot in (0, 1, 3, 2):
         if slot:
             wait_values(1, slot)
         stack_taps(slot, 1, scale)
+    middle_sends = list(sends)
+    sends.clear()
     convolve(1)
+    for copy in middle_sends:
+        copy.wait_send()
+    drain_next(0)
     result = pack_latent(lat) + collect(1)
     for f in range(FRAMES):
         rest = result[:, FRAMES * MAIN :]
@@ -521,15 +543,8 @@
         frame = jnp.concatenate([result[:, f * MAIN : (f + 1) * MAIN], rest], axis=1)
         out_ref[f] = frame[:, : ROWS * COLS].astype(BF16)
 
-    for copy in sends:
-        copy.wait_send()
-
-    @pl.when(t < sections - 1)
-    def _():
-        for j in range(2):
-            for e in range(SIDE):
-                for part in range(2):
-                    next_copy(j, e, part).wait_send()
+    drain()
+    drain_next(1)
 
 
 def block(sections, latent, gain_one, weight_one, bias_one, gain_two, weight_two, bias_two):

time: 36.1 us -> 36.2 us (level)
  no operation moved by 1% of the time
where the time goes in v7:
time: 36.2 us; the launch traced here: 36 us
  Pallas kernels  35.4 us (98%)
  local copies, waits for them, and re-layouts  0.64 us (2%)
    pallas_call x1, Pallas kernels, block(): pl.pallas_call(functools.partial(kernel, sections, chans), out_shape=jax....  35.4 us

profile of v7, /device:TPU:1, one launch (start us, length us, event | category | flops | bytes accessed | tf_op | source)
XLA Modules:
  0.0 36.0 jit_solution(6053352258726749677)
XLA Ops:
  0.0 35.4 %shard_map.73 = bf16[3,24,416]{2,1,0:T(8,128)(2,1)S(1)} custom-call(bf16[3,24,416]{2,1,0:T(8,128)(2,1)} %bitcast.11, bf16[27,24,384]{2,1,0:T(8,128)(2,1)} %bitcast.9, bf16[27,24,384]{2,1,0:T(8,128)(2,1)} %bitcast.10, f32[1,24]{1,0:T(1,128)} %bitcast.12, f32[1,24]{1,0:T(1,128)} %bitcast.13, f32[1,24]{1,0:T(1,128)} %bitcast.14, f32[1,24]{1,0:T(1,128)} %bitcast.15), custom_call_target="tpu_custom_call" | custom-call | tf_op jit(solution)/shard_map/pallas_call | solution.py:555
  35.4 0.6 %copy.9 = bf16[24,3,416]{2,0,1:T(8,128)(2,1)} copy(bf16[24,3,416]{2,0,1:T(8,128)(2,1)S(1)} %bitcast.8) | data formatting | bytes 119808

commit v8 on v7

--- a/solution.py
+++ b/solution.py
@@ -488,12 +488,12 @@
         before_far[...] = jnp.zeros(before_far.shape, BF16)
         before_near[...] = jnp.zeros(before_near.shape, BF16)
 
-    turn_weights(0)
     pl.semaphore_wait(barrier, 6 + jnp.where(t > 0, 1, 0))
     for d in (1, 2, 3):
         tell(ready, (t, SIDE * y + shifted(x, d)))
     send_squares(0, False)
     send_values(0, far_first)
+    turn_weights(0)
     send_weights(0, far)
     pl.semaphore_wait(ready, 3)
     send_squares(0, True)

time: 36.2 us -> 36 us (level)
  no operation moved by 1% of the time
where the time goes in v8:
time: 36 us; the launch traced here: 35.9 us
  Pallas kernels  35.3 us (98%)
  local copies, waits for them, and re-layouts  0.64 us (2%)
    pallas_call x1, Pallas kernels, block(): pl.pallas_call(functools.partial(kernel, sections, chans), out_shape=jax....  35.3 us

profile of v8, /device:TPU:1, one launch (start us, length us, event | category | flops | bytes accessed | tf_op | source)
XLA Modules:
  0.0 35.9 jit_solution(5534973815948494739)
XLA Ops:
  0.0 35.3 %shard_map.73 = bf16[3,24,416]{2,1,0:T(8,128)(2,1)S(1)} custom-call(bf16[3,24,416]{2,1,0:T(8,128)(2,1)} %bitcast.11, bf16[27,24,384]{2,1,0:T(8,128)(2,1)} %bitcast.9, bf16[27,24,384]{2,1,0:T(8,128)(2,1)} %bitcast.10, f32[1,24]{1,0:T(1,128)} %bitcast.12, f32[1,24]{1,0:T(1,128)} %bitcast.13, f32[1,24]{1,0:T(1,128)} %bitcast.14, f32[1,24]{1,0:T(1,128)} %bitcast.15), custom_call_target="tpu_custom_call" | custom-call | tf_op jit(solution)/shard_map/pallas_call | solution.py:555
  35.3 0.6 %copy.9 = bf16[24,3,416]{2,0,1:T(8,128)(2,1)} copy(bf16[24,3,416]{2,0,1:T(8,128)(2,1)S(1)} %bitcast.8) | data formatting | bytes 119808

commit v9 on v8

--- a/solution.py
+++ b/solution.py
@@ -187,7 +187,7 @@
             device_id_type=pl.DeviceIdType.MESH,
         )
 
-    near, far, far_first, next_order = (1, 3), (2,), (2, 1, 3), (2, 1, 3, 0)
+    near, far, far_first, next_order = (1, 3), (2,), (1, 2, 3), (2, 1, 3, 0)
 
     loads = [
         pltpu.make_async_copy(lat_hbm, lat, local_sem.at[0]),

time: 36 us -> 36.3 us (level)
  no operation moved by 1% of the time
where the time goes in v9:
time: 36.3 us; the launch traced here: 36.2 us
  Pallas kernels  35.5 us (98%)
  local copies, waits for them, and re-layouts  0.64 us (2%)
    pallas_call x1, Pallas kernels, block(): pl.pallas_call(functools.partial(kernel, sections, chans), out_shape=jax....  35.5 us

profile of v9, /device:TPU:1, one launch (start us, length us, event | category | flops | bytes accessed | tf_op | source)
XLA Modules:
  0.0 36.2 jit_solution(8120588066021281478)
XLA Ops:
  0.0 35.5 %shard_map.73 = bf16[3,24,416]{2,1,0:T(8,128)(2,1)S(1)} custom-call(bf16[3,24,416]{2,1,0:T(8,128)(2,1)} %bitcast.11, bf16[27,24,384]{2,1,0:T(8,128)(2,1)} %bitcast.9, bf16[27,24,384]{2,1,0:T(8,128)(2,1)} %bitcast.10, f32[1,24]{1,0:T(1,128)} %bitcast.12, f32[1,24]{1,0:T(1,128)} %bitcast.13, f32[1,24]{1,0:T(1,128)} %bitcast.14, f32[1,24]{1,0:T(1,128)} %bitcast.15), custom_call_target="tpu_custom_call" | custom-call | tf_op jit(solution)/shard_map/pallas_call | solution.py:555
  35.5 0.6 %copy.9 = bf16[24,3,416]{2,0,1:T(8,128)(2,1)} copy(bf16[24,3,416]{2,0,1:T(8,128)(2,1)S(1)} %bitcast.8) | data formatting | bytes 119808
